TPU v7x, 512 devices: a whole 4x4x16 slice. The times are simulated.
512 devices in a mesh: wide: 32 (over z_hi, x, core), mid: 4 (over y), narrow: 4 (over z_lo).
Axes of the slice: x: 4, y: 4, z: 16 (z_hi: 4, z_lo: 4; z = z_hi * 4 + z_lo), core: 2. Of those that a mesh axis runs over, the one named last changes fastest.
Arguments:
- mold_temp: float32 [512, 64, 512], P('wide', 'mid', 'narrow'), may hold values from -1 to 0.5
- capacity: float32 [512, 64, 512], P('wide', 'mid', 'narrow'), may hold values from 0.25 to 4
- melt_temp: float32 [64, 65536], P(None, ('wide', 'mid', 'narrow')), may hold values from 0.5 to 2.5
- log_pressure: float32 [64, 65536], P(None, ('wide', 'mid', 'narrow')), may hold values from 0 to 1.5
- target_volume: float32 [64, 65536], P(None, ('wide', 'mid', 'narrow')), may hold values from 0.7 to 1.4
- inflow: float32 [64, 65536], P(None, ('wide', 'mid', 'narrow')), may hold values from -3 to 3
- self_blocks: bfloat16 [64, 64, 65536], P(None, None, ('wide', 'mid', 'narrow'))
- link_blocks: bfloat16 [2, 64, 64, 65536], P(None, None, None, ('wide', 'mid', 'narrow')), may hold values from -0.119628906 to 0.119628906
- link_columns: int32 [2, 65536], P(None, ('wide', 'mid', 'narrow')), may hold values from 0 to 127
- wall_owner: int32 [65536], P(('wide', 'mid', 'narrow')), may hold values from 0 to 31, as said below
- wall_slot: int32 [65536], P(('wide', 'mid', 'narrow')), may hold values from 0 to 31
- transfer_coef: float32 [64, 65536], P(None, ('wide', 'mid', 'narrow')), may hold values from 0.2 to 1
Outputs:
- mold_out: float32 [512, 64, 512], P('wide', 'mid', 'narrow')
- pressure: float32 [64, 65536], P(None, ('wide', 'mid', 'narrow'))
- shrinkage: float32 [64, 65536], P(None, ('wide', 'mid', 'narrow'))
Inputs may be any that keep to these rules, and one draw needn't show every extreme that they name: `wall_owner`: in each device's 128 blocks no owner is named more than 16 times and one owner exactly 16 times; that owner is the same on all devices with the same mid and narrow indices. `link_columns`: indices among the 128 blocks of the same device.
All inputs are finite; a program needn't handle non-finite values.
Results may differ from a plain program's by a relative error of at most 0.01.
Values sent between devices are 32-bit elements; how exact they have to be, the bound alone decides.
A program may use at most 64 MiB of HBM per device.

v0:
```python
import jax
import jax.numpy as jnp
from jax import lax
from jax.sharding import PartitionSpec as P

BLOCK = 64
ITERS = 2
SWEEPS = 4
INNER = 2


CONDUCT = 1.0
COOLING = 0.5
TAIT_C = 0.3
EXPAND = 0.25
BULK_BASE = 0.5
BULK_SLOPE = 0.3


def padded_2(shard, sides, width):
    for axis, dim in sides:
        size, length = (lax.axis_size(axis), shard.shape[dim])
        up = [(i, (i + 1) % size) for i in range(size - 1)]
        down = [(j, i) for i, j in up]
        last = lax.slice_in_dim(shard, length - width, length, axis=dim)
        leading = lax.slice_in_dim(shard, 0, width, axis=dim)
        before = lax.ppermute(last, axis, up)
        after = lax.ppermute(leading, axis, down)
        shard = jnp.concatenate([before, shard, after], axis=dim)
    return shard


def beside_of(padded):
    beside = padded[2:, 1:-1, 1:-1] + padded[:-2, 1:-1, 1:-1]
    beside = beside + padded[1:-1, 2:, 1:-1] + padded[1:-1, :-2, 1:-1]
    beside = beside + padded[1:-1, 1:-1, 2:] + padded[1:-1, 1:-1, :-2]
    return beside


def block_apply(self_blocks, link_blocks, link_columns, values):
    nearby = values[:, link_columns]
    first = jnp.einsum("ijb,jb->ib", self_blocks, values, preferred_element_type=jnp.float32)
    second = jnp.einsum("nijb,jnb->ib", link_blocks, nearby, preferred_element_type=jnp.float32)
    return first + second


def newton(state, melt, target_volume, inflow, self_blocks, link_blocks, link_columns, self_diag):
    bulk_modulus = BULK_BASE * jnp.exp(-BULK_SLOPE * melt)
    growth = jnp.exp(state)
    pressure = bulk_modulus * (growth - 1.0)
    base_volume = jnp.exp(EXPAND * melt)
    volume = base_volume * (1.0 - TAIT_C * state)
    rounded = pressure.astype(jnp.bfloat16)
    residual = (
        block_apply(self_blocks, link_blocks, link_columns, rounded)
        + (target_volume - volume)
        - inflow
    )
    press_slope = bulk_modulus * growth
    diagonal = self_diag * press_slope + TAIT_C * base_volume
    update = -residual / diagonal
    for repeat in range(INNER):
        weighted = (press_slope * update).astype(jnp.bfloat16)
        linked = block_apply(
            self_blocks, link_blocks, link_columns, weighted
        ) - self_diag * weighted.astype(jnp.float32)
        update = (-residual - linked) / diagonal
    return state + update


def per_device(
    mold_temp,
    capacity,
    melt_temp,
    log_pressure,
    target_volume,
    inflow,
    self_blocks,
    link_blocks,
    link_columns,
    wall_owner,
    wall_slot,
    transfer_coef,
):
    width, height, depth = mold_temp.shape
    faces = height * depth // BLOCK
    groups = lax.axis_size("wide")
    self_diag = jnp.diagonal(self_blocks, axis1=0, axis2=1).T.astype(jnp.float32)
    table_column = wall_owner * faces + wall_slot
    field = mold_temp
    melt = melt_temp
    state = log_pressure
    for iteration in range(ITERS):
        columns = field[0].reshape(faces, BLOCK).T
        table = lax.all_gather(columns, "wide", axis=1, tiled=True)
        wall = table[:, table_column]
        flux = transfer_coef * (melt - wall)
        melt = melt - COOLING * flux
        spread = jnp.zeros((BLOCK, groups * faces), jnp.float32).at[:, table_column].add(flux)
        source_columns = lax.psum_scatter(spread, "wide", scatter_dimension=1, tiled=True)
        wall_layer = source_columns.T.reshape(height, depth)
        state = newton(
            state, melt, target_volume, inflow, self_blocks, link_blocks, link_columns, self_diag
        )
        source = jnp.zeros_like(field).at[0].set(wall_layer)
        for sweep_index in range(SWEEPS):
            padded = padded_2(field, (("wide", 0), ("mid", 1), ("narrow", 2)), 1)
            field = (capacity * mold_temp + source + CONDUCT * beside_of(padded)) / (
                capacity + 6.0 * CONDUCT
            )
    pressure = BULK_BASE * jnp.exp(-BULK_SLOPE * melt) * (jnp.exp(state) - 1.0)
    shrinkage = 1.0 - jnp.exp(EXPAND * melt) * (1.0 - TAIT_C * state)
    return (field, pressure, shrinkage)


def solution(mesh):
    return jax.shard_map(
        per_device,
        mesh=mesh,
        in_specs=(
            P("wide", "mid", "narrow"),
            P("wide", "mid", "narrow"),
            P(None, ("wide", "mid", "narrow")),
            P(None, ("wide", "mid", "narrow")),
            P(None, ("wide", "mid", "narrow")),
            P(None, ("wide", "mid", "narrow")),
            P(None, None, ("wide", "mid", "narrow")),
            P(None, None, None, ("wide", "mid", "narrow")),
            P(None, ("wide", "mid", "narrow")),
            P(("wide", "mid", "narrow")),
            P(("wide", "mid", "narrow")),
            P(None, ("wide", "mid", "narrow")),
        ),
        out_specs=(
            P("wide", "mid", "narrow"),
            P(None, ("wide", "mid", "narrow")),
            P(None, ("wide", "mid", "narrow")),
        ),
        check_vma=False,
    )
```

profile of v0, /device:TPU:7, one launch (start us, length us, event | category | flops | bytes accessed | tf_op | source)
XLA Modules:
  0.0 588.1 jit_solution(14643785646176029502)
XLA Ops:
  8.0 9.3 %collective-permute-start.1 = (f32[1,16,128]{2,1,0:T(8,128)S(1)}, f32[1,16,128]{2,1,0:T(8,128)S(1)}, u32[]{:S(2)}, u32[]{:S(2)}) collective-permute-start(f32[1,16,128]{2,1,0:T(8,128)S(1)} %get-tuple-element.97), channel_id=1, source_target_pairs={{0,16},{16,32},{32,48},{48,64},{64,80},{80,96},{96,112},{112,128},... | collective-permute-start | bytes 24584 | tf_op jit(solution)/shard_map/ppermute | solution.py:27
  17.3 1.9 collective-permute-start
  19.3 49.4 %all_gather.6 = f32[64,1024]{0,1:T(8,128)S(1)} all-gather(f32[64,32]{0,1:T(8,128)S(1)} %bitcast.135), channel_id=1, replica_groups=mesh['wide'=32,'mid'=4,'narrow'=4] {'wide'}, dimensions={1}, use_global_device_ids=true | all-gather | bytes 270336 | tf_op jit(solution)/shard_map/all_gather | solution.py:95
  70.7 1.5 bitcast_convert_fusion.5
  72.2 1.8 scatter_custom_fusion
  75.7 4.0 collective-permute-start.3
  83.0 4.5 collective-permute-start.5
  88.8 96.3 %reduce-scatter.3.cloned.1.call-done = f32[64,32]{0,1:T(8,128)} async-done(((f32[64,1024]{0,1:T(8,128)}), f32[64,32]{0,1:T(8,128)}) %reduce-scatter.3.cloned.1.call-update) | async-done | bytes 8208 | tf_op jit(solution)/shard_map/reduce_scatter | solution.py:100
  187.2 1.7 fusion.67
  188.9 4.3 collective-permute-start.6
  193.2 7.3 %collective-permute-start.7 = (f32[1,16,128]{2,1,0:T(8,128)S(1)}, f32[1,16,128]{2,1,0:T(8,128)S(1)}, u32[]{:S(2)}, u32[]{:S(2)}) collective-permute-start(f32[1,16,128]{2,1,0:T(8,128)S(1)} %get-tuple-element.93), channel_id=1, source_target_pairs={{0,16},{16,32},{32,48},{48,64},{64,80},{80,96},{96,112},{112,128},... | collective-permute-start | bytes 24584 | tf_op jit(solution)/shard_map/ppermute | solution.py:27
  200.5 2.0 fusion
  203.8 4.0 collective-permute-start.9
  209.7 3.0 collective-permute-start.11
  215.4 4.2 collective-permute-done.10
  219.6 1.7 fusion.60
  222.6 1.9 collective-permute-start.12
  224.5 11.3 %collective-permute-start.13 = (f32[1,16,128]{2,1,0:T(8,128)}, f32[1,16,128]{2,1,0:T(8,128)}, u32[]{:S(2)}, u32[]{:S(2)}) collective-permute-start(f32[1,16,128]{2,1,0:T(8,128)} %get-tuple-element.91), channel_id=1, source_target_pairs={{0,16},{16,32},{32,48},{48,64},{64,80},{80,96},{96,112},{112,128},... | collective-permute-start | bytes 24584 | tf_op jit(solution)/shard_map/ppermute | solution.py:27
  235.8 1.5 bitcast_convert_fusion.4
  238.1 2.2 gather_fusion.4
  240.3 1.5 copy.120
  244.1 4.5 collective-permute-start.15
  251.0 2.2 collective-permute-start.17
  256.0 3.8 collective-permute-done.16
  262.1 1.9 collective-permute-start.18
  264.0 9.7 %collective-permute-start.19 = (f32[1,16,128]{2,1,0:T(8,128)}, f32[1,16,128]{2,1,0:T(8,128)}, u32[]{:S(2)}, u32[]{:S(2)}) collective-permute-start(f32[1,16,128]{2,1,0:T(8,128)} %get-tuple-element.89), channel_id=1, source_target_pairs={{0,16},{16,32},{32,48},{48,64},{64,80},{80,96},{96,112},{112,128},... | collective-permute-start | bytes 24584 | tf_op jit(solution)/shard_map/ppermute | solution.py:27
  274.3 1.4 copy.35
  275.8 2.2 gather_fusion.5
  278.0 1.5 copy.122
  281.8 4.0 collective-permute-start.21
  285.8 2.0 fusion.2
  288.7 3.2 collective-permute-start.23
  294.7 3.8 collective-permute-done.22
  301.5 1.9 collective-permute-start.24
  303.4 52.6 %all_gather.7 = f32[64,1024]{0,1:T(8,128)} all-gather(f32[64,32]{0,1:T(8,128)S(1)} %bitcast.134), channel_id=1, replica_groups=mesh['wide'=32,'mid'=4,'narrow'=4] {'wide'}, dimensions={1}, use_global_device_ids=true | all-gather | bytes 270336 | tf_op jit(solution)/shard_map/all_gather | solution.py:95
  356.1 1.8 gather_fusion.1
  358.0 7.9 %collective-permute-start.25 = (f32[1,16,128]{2,1,0:T(8,128)}, f32[1,16,128]{2,1,0:T(8,128)}, u32[]{:S(2)}, u32[]{:S(2)}) collective-permute-start(f32[1,16,128]{2,1,0:T(8,128)} %get-tuple-element.87), channel_id=1, source_target_pairs={{0,16},{16,32},{32,48},{48,64},{64,80},{80,96},{96,112},{112,128},... | collective-permute-start | bytes 24584 | tf_op jit(solution)/shard_map/ppermute | solution.py:27
  365.9 1.5 bitcast_convert_fusion.2
  368.2 2.1 scatter_custom_fusion.1
  370.4 1.6 gather_fusion.6
  372.0 1.6 copy.124
  375.8 4.0 collective-permute-start.27
  379.8 2.0 fusion.3
  383.4 2.0 collective-permute-start.29
  386.7 86.7 %reduce-scatter.5.cloned.1.call-done = f32[64,32]{0,1:T(8,128)} async-done(((f32[64,1024]{0,1:T(8,128)}), f32[64,32]{0,1:T(8,128)}) %reduce-scatter.5.cloned.1.call-update) | async-done | bytes 8208 | tf_op jit(solution)/shard_map/reduce_scatter | solution.py:100
  476.9 4.3 collective-permute-start.30
  481.3 7.3 %collective-permute-start.31 = (f32[1,16,128]{2,1,0:T(8,128)S(1)}, f32[1,16,128]{2,1,0:T(8,128)S(1)}, u32[]{:S(2)}, u32[]{:S(2)}) collective-permute-start(f32[1,16,128]{2,1,0:T(8,128)S(1)} %get-tuple-element.85), channel_id=1, source_target_pairs={{0,16},{16,32},{32,48},{48,64},{64,80},{80,96},{96,112},{112,128},... | collective-permute-start | bytes 24584 | tf_op jit(solution)/shard_map/ppermute | solution.py:27
  491.6 4.6 collective-permute-start.33
  497.4 1.6 gather_fusion.7
  499.0 1.6 copy.126
  501.8 2.3 collective-permute-start.35
  507.0 4.3 collective-permute-done.34
  512.4 1.9 collective-permute-start.36
  514.3 11.5 %collective-permute-start.37 = (f32[1,16,128]{2,1,0:T(8,128)S(1)}, f32[1,16,128]{2,1,0:T(8,128)S(1)}, u32[]{:S(2)}, u32[]{:S(2)}) collective-permute-start(f32[1,16,128]{2,1,0:T(8,128)S(1)} %get-tuple-element.83), channel_id=1, source_target_pairs={{0,16},{16,32},{32,48},{48,64},{64,80},{80,96},{96,112},{112,128},... | collective-permute-start | bytes 24584 | tf_op jit(solution)/shard_map/ppermute | solution.py:27
  528.5 4.6 collective-permute-start.39
  534.3 1.6 gather_fusion.8
  535.9 1.6 copy.128
  538.6 2.8 collective-permute-start.41
  544.3 4.0 collective-permute-done.40
  549.4 1.9 collective-permute-start.42
  551.3 12.2 %collective-permute-start.43 = (f32[1,16,128]{2,1,0:T(8,128)S(1)}, f32[1,16,128]{2,1,0:T(8,128)S(1)}, u32[]{:S(2)}, u32[]{:S(2)}) collective-permute-start(f32[1,16,128]{2,1,0:T(8,128)S(1)} %get-tuple-element.81), channel_id=1, source_target_pairs={{0,16},{16,32},{32,48},{48,64},{64,80},{80,96},{96,112},{112,128},... | collective-permute-start | bytes 24584 | tf_op jit(solution)/shard_map/ppermute | solution.py:27
  565.6 4.0 collective-permute-start.45
  570.5 3.2 collective-permute-start.47
  576.6 3.8 collective-permute-done.46
  (266 shorter events, 72.3 us)
Async XLA Ops:
  7.2 67.0 %copy-start.19 = (f32[16,16,128]{2,1,0:T(8,128)S(1)}, f32[16,16,128]{2,1,0:T(8,128)}, u32[]{:S(2)}) copy-start(f32[16,16,128]{2,1,0:T(8,128)} %param.16) | copy-start | bytes 393220
  7.2 66.9 %copy-start.60 = (s32[2,128]{1,0:T(2,128)S(1)}, s32[2,128]{1,0:T(2,128)}, u32[]{:S(2)}) copy-start(s32[2,128]{1,0:T(2,128)} %param.24) | copy-start | bytes 3076
  7.2 67.0 %copy-start.2 = (f32[16,16,128]{2,1,0:T(8,128)S(1)}, f32[16,16,128]{2,1,0:T(8,128)}, u32[]{:S(2)}) copy-start(f32[16,16,128]{2,1,0:T(8,128)} %param.17) | copy-start | bytes 393220
  7.2 177.9 %reduce-scatter.3.cloned.1.call-start = ((), (), s32[]{:S(2)}) async-start(), calls=%async_computation.2 | async-start | bytes 540672 | tf_op jit(solution)/shard_map/reduce_scatter | solution.py:100
  8.0 66.1 %collective-permute-start.1 = (f32[1,16,128]{2,1,0:T(8,128)S(1)}, f32[1,16,128]{2,1,0:T(8,128)S(1)}, u32[]{:S(2)}, u32[]{:S(2)}) collective-permute-start(f32[1,16,128]{2,1,0:T(8,128)S(1)} %get-tuple-element.97), channel_id=1, source_target_pairs={{0,16},{16,32},{32,48},{48,64},{64,80},{80,96},{96,112},{112,128},... | collective-permute-start | bytes 24584 | tf_op jit(solution)/shard_map/ppermute | solution.py:27
  17.3 56.9 %collective-permute-start = (f32[1,16,128]{2,1,0:T(8,128)S(1)}, f32[1,16,128]{2,1,0:T(8,128)S(1)}, u32[]{:S(2)}, u32[]{:S(2)}) collective-permute-start(f32[1,16,128]{2,1,0:T(8,128)S(1)} %get-tuple-element.98), channel_id=1, source_target_pairs={{16,0},{32,16},{48,32},{64,48},{80,64},{96,80},{112,96},{128,112},... | collective-permute-start | bytes 24584 | tf_op jit(solution)/shard_map/ppermute | solution.py:28
  74.0 126.5 %copy-start = (bf16[2,64,64,128]{3,2,1,0:T(8,128)(2,1)S(1)}, bf16[2,64,64,128]{3,2,1,0:T(8,128)(2,1)}, u32[]{:S(2)}) copy-start(bf16[2,64,64,128]{3,2,1,0:T(8,128)(2,1)} %param.23) | copy-start | bytes 6291460
  74.0 399.4 %reduce-scatter.5.cloned.1.call-start = ((), (), s32[]{:S(2)}) async-start(), calls=%async_computation.3 | async-start | bytes 540672 | tf_op jit(solution)/shard_map/reduce_scatter | solution.py:100
  74.3 7.2 %collective-permute-start.2 = (f32[18,1,128]{2,1,0:T(1,128)S(1)}, f32[18,1,128]{2,1,0:T(1,128)S(1)}, u32[]{:S(2)}, u32[]{:S(2)}) collective-permute-start(f32[18,1,128]{2,1,0:T(1,128)S(1)} %get-tuple-element.80), channel_id=1, source_target_pairs={{4,0},{8,4},{12,8},{5,1},{9,5},{13,9},{6,2},{10,6},{14,10},{7,3},{... | collective-permute-start | bytes 27656 | tf_op jit(solution)/shard_map/ppermute | solution.py:28
  75.7 5.7 collective-permute-start.3
  82.1 125.7 %copy-start.1 = (bf16[64,64,128]{2,1,0:T(8,128)(2,1)S(1)}, bf16[64,64,128]{2,1,0:T(8,128)(2,1)}, u32[]{:S(2)}) copy-start(bf16[64,64,128]{2,1,0:T(8,128)(2,1)} %param.22) | copy-start | bytes 3145732
  83.0 104.2 %collective-permute-start.5 = (f32[18,18,1]{2,1,0:T(8,128)}, f32[18,18,1]{2,1,0:T(8,128)}, u32[]{:S(2)}, u32[]{:S(2)}) collective-permute-start(f32[18,18,1]{2,1,0:T(8,128)} %get-tuple-element.64), channel_id=1, source_target_pairs={{0,1},{1,2},{2,3},{4,5},{5,6},{6,7},{8,9},{9,10},{10,11},{12,13},{... | collective-permute-start | bytes 3896 | tf_op jit(solution)/shard_map/ppermute | solution.py:27
  87.5 99.7 %collective-permute-start.4 = (f32[18,18,1]{2,1,0:T(8,128)}, f32[18,18,1]{2,1,0:T(8,128)}, u32[]{:S(2)}, u32[]{:S(2)}) collective-permute-start(f32[18,18,1]{2,1,0:T(8,128)} %get-tuple-element.63), channel_id=1, source_target_pairs={{1,0},{2,1},{3,2},{5,4},{6,5},{7,6},{9,8},{10,9},{11,10},{13,12},{... | collective-permute-start | bytes 3896 | tf_op jit(solution)/shard_map/ppermute | solution.py:28
  188.9 13.6 %collective-permute-start.6 = (f32[1,16,128]{2,1,0:T(8,128)S(1)}, f32[1,16,128]{2,1,0:T(8,128)S(1)}, u32[]{:S(2)}, u32[]{:S(2)}) collective-permute-start(f32[1,16,128]{2,1,0:T(8,128)S(1)} %get-tuple-element.94), channel_id=1, source_target_pairs={{16,0},{32,16},{48,32},{64,48},{80,64},{96,80},{112,96},{128,112},... | collective-permute-start | bytes 24584 | tf_op jit(solution)/shard_map/ppermute | solution.py:28
  193.2 9.3 %collective-permute-start.7 = (f32[1,16,128]{2,1,0:T(8,128)S(1)}, f32[1,16,128]{2,1,0:T(8,128)S(1)}, u32[]{:S(2)}, u32[]{:S(2)}) collective-permute-start(f32[1,16,128]{2,1,0:T(8,128)S(1)} %get-tuple-element.93), channel_id=1, source_target_pairs={{0,16},{16,32},{32,48},{48,64},{64,80},{80,96},{96,112},{112,128},... | collective-permute-start | bytes 24584 | tf_op jit(solution)/shard_map/ppermute | solution.py:27
  202.5 6.3 %collective-permute-start.8 = (f32[18,1,128]{2,1,0:T(1,128)S(1)}, f32[18,1,128]{2,1,0:T(1,128)S(1)}, u32[]{:S(2)}, u32[]{:S(2)}) collective-permute-start(f32[18,1,128]{2,1,0:T(1,128)S(1)} %get-tuple-element.78), channel_id=1, source_target_pairs={{4,0},{8,4},{12,8},{5,1},{9,5},{13,9},{6,2},{10,6},{14,10},{7,3},{... | collective-permute-start | bytes 27656 | tf_op jit(solution)/shard_map/ppermute | solution.py:28
  203.8 5.0 collective-permute-start.9
  209.7 5.7 collective-permute-start.11
  212.6 7.0 %collective-permute-start.10 = (f32[18,18,1]{2,1,0:T(8,128)}, f32[18,18,1]{2,1,0:T(8,128)}, u32[]{:S(2)}, u32[]{:S(2)}) collective-permute-start(f32[18,18,1]{2,1,0:T(8,128)} %get-tuple-element.61), channel_id=1, source_target_pairs={{1,0},{2,1},{3,2},{5,4},{6,5},{7,6},{9,8},{10,9},{11,10},{13,12},{... | collective-permute-start | bytes 3896 | tf_op jit(solution)/shard_map/ppermute | solution.py:28
  222.6 19.3 %collective-permute-start.12 = (f32[1,16,128]{2,1,0:T(8,128)}, f32[1,16,128]{2,1,0:T(8,128)}, u32[]{:S(2)}, u32[]{:S(2)}) collective-permute-start(f32[1,16,128]{2,1,0:T(8,128)} %get-tuple-element.92), channel_id=1, source_target_pairs={{16,0},{32,16},{48,32},{64,48},{80,64},{96,80},{112,96},{128,112},... | collective-permute-start | bytes 24584 | tf_op jit(solution)/shard_map/ppermute | solution.py:28
  224.5 17.4 %collective-permute-start.13 = (f32[1,16,128]{2,1,0:T(8,128)}, f32[1,16,128]{2,1,0:T(8,128)}, u32[]{:S(2)}, u32[]{:S(2)}) collective-permute-start(f32[1,16,128]{2,1,0:T(8,128)} %get-tuple-element.91), channel_id=1, source_target_pairs={{0,16},{16,32},{32,48},{48,64},{64,80},{80,96},{96,112},{112,128},... | collective-permute-start | bytes 24584 | tf_op jit(solution)/shard_map/ppermute | solution.py:27
  242.8 7.3 %collective-permute-start.14 = (f32[18,1,128]{2,1,0:T(1,128)S(1)}, f32[18,1,128]{2,1,0:T(1,128)S(1)}, u32[]{:S(2)}, u32[]{:S(2)}) collective-permute-start(f32[18,1,128]{2,1,0:T(1,128)S(1)} %get-tuple-element.76), channel_id=1, source_target_pairs={{4,0},{8,4},{12,8},{5,1},{9,5},{13,9},{6,2},{10,6},{14,10},{7,3},{... | collective-permute-start | bytes 27656 | tf_op jit(solution)/shard_map/ppermute | solution.py:28
  244.1 6.0 %collective-permute-start.15 = (f32[18,1,128]{2,1,0:T(1,128)S(1)}, f32[18,1,128]{2,1,0:T(1,128)S(1)}, u32[]{:S(2)}, u32[]{:S(2)}) collective-permute-start(f32[18,1,128]{2,1,0:T(1,128)S(1)} %get-tuple-element.75), channel_id=1, source_target_pairs={{0,4},{4,8},{8,12},{1,5},{5,9},{9,13},{2,6},{6,10},{10,14},{3,7},{... | collective-permute-start | bytes 27656 | tf_op jit(solution)/shard_map/ppermute | solution.py:27
  251.0 5.0 collective-permute-start.17
  253.2 6.7 %collective-permute-start.16 = (f32[18,18,1]{2,1,0:T(8,128)S(1)}, f32[18,18,1]{2,1,0:T(8,128)S(1)}, u32[]{:S(2)}, u32[]{:S(2)}) collective-permute-start(f32[18,18,1]{2,1,0:T(8,128)S(1)} %get-tuple-element.59), channel_id=1, source_target_pairs={{1,0},{2,1},{3,2},{5,4},{6,5},{7,6},{9,8},{10,9},{11,10},{13,12},{... | collective-permute-start | bytes 3896 | tf_op jit(solution)/shard_map/ppermute | solution.py:28
  262.1 17.5 %collective-permute-start.18 = (f32[1,16,128]{2,1,0:T(8,128)}, f32[1,16,128]{2,1,0:T(8,128)}, u32[]{:S(2)}, u32[]{:S(2)}) collective-permute-start(f32[1,16,128]{2,1,0:T(8,128)} %get-tuple-element.90), channel_id=1, source_target_pairs={{16,0},{32,16},{48,32},{64,48},{80,64},{96,80},{112,96},{128,112},... | collective-permute-start | bytes 24584 | tf_op jit(solution)/shard_map/ppermute | solution.py:28
  264.0 15.6 %collective-permute-start.19 = (f32[1,16,128]{2,1,0:T(8,128)}, f32[1,16,128]{2,1,0:T(8,128)}, u32[]{:S(2)}, u32[]{:S(2)}) collective-permute-start(f32[1,16,128]{2,1,0:T(8,128)} %get-tuple-element.89), channel_id=1, source_target_pairs={{0,16},{16,32},{32,48},{48,64},{64,80},{80,96},{96,112},{112,128},... | collective-permute-start | bytes 24584 | tf_op jit(solution)/shard_map/ppermute | solution.py:27
  280.5 7.3 %collective-permute-start.20 = (f32[18,1,128]{2,1,0:T(1,128)S(1)}, f32[18,1,128]{2,1,0:T(1,128)S(1)}, u32[]{:S(2)}, u32[]{:S(2)}) collective-permute-start(f32[18,1,128]{2,1,0:T(1,128)S(1)} %get-tuple-element.74), channel_id=1, source_target_pairs={{4,0},{8,4},{12,8},{5,1},{9,5},{13,9},{6,2},{10,6},{14,10},{7,3},{... | collective-permute-start | bytes 27656 | tf_op jit(solution)/shard_map/ppermute | solution.py:28
  281.8 6.0 %collective-permute-start.21 = (f32[18,1,128]{2,1,0:T(1,128)S(1)}, f32[18,1,128]{2,1,0:T(1,128)S(1)}, u32[]{:S(2)}, u32[]{:S(2)}) collective-permute-start(f32[18,1,128]{2,1,0:T(1,128)S(1)} %get-tuple-element.73), channel_id=1, source_target_pairs={{0,4},{4,8},{8,12},{1,5},{5,9},{9,13},{2,6},{6,10},{10,14},{3,7},{... | collective-permute-start | bytes 27656 | tf_op jit(solution)/shard_map/ppermute | solution.py:27
  288.7 6.0 %collective-permute-start.23 = (f32[18,18,1]{2,1,0:T(8,128)S(1)}, f32[18,18,1]{2,1,0:T(8,128)S(1)}, u32[]{:S(2)}, u32[]{:S(2)}) collective-permute-start(f32[18,18,1]{2,1,0:T(8,128)S(1)} %get-tuple-element.58), channel_id=1, source_target_pairs={{0,1},{1,2},{2,3},{4,5},{5,6},{6,7},{8,9},{9,10},{10,11},{12,13},{... | collective-permute-start | bytes 3896 | tf_op jit(solution)/shard_map/ppermute | solution.py:27
  291.9 6.7 %collective-permute-start.22 = (f32[18,18,1]{2,1,0:T(8,128)S(1)}, f32[18,18,1]{2,1,0:T(8,128)S(1)}, u32[]{:S(2)}, u32[]{:S(2)}) collective-permute-start(f32[18,18,1]{2,1,0:T(8,128)S(1)} %get-tuple-element.57), channel_id=1, source_target_pairs={{1,0},{2,1},{3,2},{5,4},{6,5},{7,6},{9,8},{10,9},{11,10},{13,12},{... | collective-permute-start | bytes 3896 | tf_op jit(solution)/shard_map/ppermute | solution.py:28
  301.5 72.1 %collective-permute-start.24 = (f32[1,16,128]{2,1,0:T(8,128)}, f32[1,16,128]{2,1,0:T(8,128)}, u32[]{:S(2)}, u32[]{:S(2)}) collective-permute-start(f32[1,16,128]{2,1,0:T(8,128)} %get-tuple-element.88), channel_id=1, source_target_pairs={{16,0},{32,16},{48,32},{64,48},{80,64},{96,80},{112,96},{128,112},... | collective-permute-start | bytes 24584 | tf_op jit(solution)/shard_map/ppermute | solution.py:28
  358.0 15.6 %collective-permute-start.25 = (f32[1,16,128]{2,1,0:T(8,128)}, f32[1,16,128]{2,1,0:T(8,128)}, u32[]{:S(2)}, u32[]{:S(2)}) collective-permute-start(f32[1,16,128]{2,1,0:T(8,128)} %get-tuple-element.87), channel_id=1, source_target_pairs={{0,16},{16,32},{32,48},{48,64},{64,80},{80,96},{96,112},{112,128},... | collective-permute-start | bytes 24584 | tf_op jit(solution)/shard_map/ppermute | solution.py:27
  374.5 7.3 %collective-permute-start.26 = (f32[18,1,128]{2,1,0:T(1,128)S(1)}, f32[18,1,128]{2,1,0:T(1,128)S(1)}, u32[]{:S(2)}, u32[]{:S(2)}) collective-permute-start(f32[18,1,128]{2,1,0:T(1,128)S(1)} %get-tuple-element.72), channel_id=1, source_target_pairs={{4,0},{8,4},{12,8},{5,1},{9,5},{13,9},{6,2},{10,6},{14,10},{7,3},{... | collective-permute-start | bytes 27656 | tf_op jit(solution)/shard_map/ppermute | solution.py:28
  375.8 6.0 %collective-permute-start.27 = (f32[18,1,128]{2,1,0:T(1,128)S(1)}, f32[18,1,128]{2,1,0:T(1,128)S(1)}, u32[]{:S(2)}, u32[]{:S(2)}) collective-permute-start(f32[18,1,128]{2,1,0:T(1,128)S(1)} %get-tuple-element.71), channel_id=1, source_target_pairs={{0,4},{4,8},{8,12},{1,5},{5,9},{9,13},{2,6},{6,10},{10,14},{3,7},{... | collective-permute-start | bytes 27656 | tf_op jit(solution)/shard_map/ppermute | solution.py:27
  383.4 92.1 %collective-permute-start.29 = (f32[18,18,1]{2,1,0:T(8,128)}, f32[18,18,1]{2,1,0:T(8,128)}, u32[]{:S(2)}, u32[]{:S(2)}) collective-permute-start(f32[18,18,1]{2,1,0:T(8,128)} %get-tuple-element.56), channel_id=1, source_target_pairs={{0,1},{1,2},{2,3},{4,5},{5,6},{6,7},{8,9},{9,10},{10,11},{12,13},{... | collective-permute-start | bytes 3896 | tf_op jit(solution)/shard_map/ppermute | solution.py:27
  385.5 90.1 %collective-permute-start.28 = (f32[18,18,1]{2,1,0:T(8,128)}, f32[18,18,1]{2,1,0:T(8,128)}, u32[]{:S(2)}, u32[]{:S(2)}) collective-permute-start(f32[18,18,1]{2,1,0:T(8,128)} %get-tuple-element.55), channel_id=1, source_target_pairs={{1,0},{2,1},{3,2},{5,4},{6,5},{7,6},{9,8},{10,9},{11,10},{13,12},{... | collective-permute-start | bytes 3896 | tf_op jit(solution)/shard_map/ppermute | solution.py:28
  476.9 12.7 %collective-permute-start.30 = (f32[1,16,128]{2,1,0:T(8,128)S(1)}, f32[1,16,128]{2,1,0:T(8,128)S(1)}, u32[]{:S(2)}, u32[]{:S(2)}) collective-permute-start(f32[1,16,128]{2,1,0:T(8,128)S(1)} %get-tuple-element.86), channel_id=1, source_target_pairs={{16,0},{32,16},{48,32},{64,48},{80,64},{96,80},{112,96},{128,112},... | collective-permute-start | bytes 24584 | tf_op jit(solution)/shard_map/ppermute | solution.py:28
  481.3 8.4 %collective-permute-start.31 = (f32[1,16,128]{2,1,0:T(8,128)S(1)}, f32[1,16,128]{2,1,0:T(8,128)S(1)}, u32[]{:S(2)}, u32[]{:S(2)}) collective-permute-start(f32[1,16,128]{2,1,0:T(8,128)S(1)} %get-tuple-element.85), channel_id=1, source_target_pairs={{0,16},{16,32},{32,48},{48,64},{64,80},{80,96},{96,112},{112,128},... | collective-permute-start | bytes 24584 | tf_op jit(solution)/shard_map/ppermute | solution.py:27
  490.3 10.4 %collective-permute-start.32 = (f32[18,1,128]{2,1,0:T(1,128)}, f32[18,1,128]{2,1,0:T(1,128)}, u32[]{:S(2)}, u32[]{:S(2)}) collective-permute-start(f32[18,1,128]{2,1,0:T(1,128)} %get-tuple-element.70), channel_id=1, source_target_pairs={{4,0},{8,4},{12,8},{5,1},{9,5},{13,9},{6,2},{10,6},{14,10},{7,3},{... | collective-permute-start | bytes 27656 | tf_op jit(solution)/shard_map/ppermute | solution.py:28
  491.6 9.1 %collective-permute-start.33 = (f32[18,1,128]{2,1,0:T(1,128)}, f32[18,1,128]{2,1,0:T(1,128)}, u32[]{:S(2)}, u32[]{:S(2)}) collective-permute-start(f32[18,1,128]{2,1,0:T(1,128)} %get-tuple-element.69), channel_id=1, source_target_pairs={{0,4},{4,8},{8,12},{1,5},{5,9},{9,13},{2,6},{6,10},{10,14},{3,7},{... | collective-permute-start | bytes 27656 | tf_op jit(solution)/shard_map/ppermute | solution.py:27
  501.8 5.2 collective-permute-start.35
  504.1 29.0 %copy-start.16 = (f32[64,128]{1,0:T(8,128)S(1)}, f32[64,128]{1,0:T(8,128)}, u32[]{:S(2)}) copy-start(f32[64,128]{1,0:T(8,128)} %get-tuple-element.39) | copy-start | bytes 98308
  504.1 29.0 %copy-start.23 = (f32[64,128]{1,0:T(8,128)S(1)}, f32[64,128]{1,0:T(8,128)}, u32[]{:S(2)}) copy-start(f32[64,128]{1,0:T(8,128)} %get-tuple-element.40) | copy-start | bytes 98308
  504.1 29.0 %copy-start.26 = (f32[64,128]{1,0:T(8,128)S(1)}, f32[64,128]{1,0:T(8,128)}, u32[]{:S(2)}) copy-start(f32[64,128]{1,0:T(8,128)} %get-tuple-element.36) | copy-start | bytes 98308
  504.1 29.0 %copy-start.33 = (bf16[64,128]{1,0:T(8,128)(2,1)S(1)}, bf16[64,128]{1,0:T(8,128)(2,1)}, u32[]{:S(2)}) copy-start(bf16[64,128]{1,0:T(8,128)(2,1)} %copy-done.32) | copy-start | bytes 49156
  504.1 7.2 %collective-permute-start.34 = (f32[18,18,1]{2,1,0:T(8,128)S(1)}, f32[18,18,1]{2,1,0:T(8,128)S(1)}, u32[]{:S(2)}, u32[]{:S(2)}) collective-permute-start(f32[18,18,1]{2,1,0:T(8,128)S(1)} %get-tuple-element.53), channel_id=1, source_target_pairs={{1,0},{2,1},{3,2},{5,4},{6,5},{7,6},{9,8},{10,9},{11,10},{13,12},{... | collective-permute-start | bytes 3896 | tf_op jit(solution)/shard_map/ppermute | solution.py:28
  512.4 13.8 %collective-permute-start.36 = (f32[1,16,128]{2,1,0:T(8,128)S(1)}, f32[1,16,128]{2,1,0:T(8,128)S(1)}, u32[]{:S(2)}, u32[]{:S(2)}) collective-permute-start(f32[1,16,128]{2,1,0:T(8,128)S(1)} %get-tuple-element.84), channel_id=1, source_target_pairs={{16,0},{32,16},{48,32},{64,48},{80,64},{96,80},{112,96},{128,112},... | collective-permute-start | bytes 24584 | tf_op jit(solution)/shard_map/ppermute | solution.py:28
  514.3 12.3 %collective-permute-start.37 = (f32[1,16,128]{2,1,0:T(8,128)S(1)}, f32[1,16,128]{2,1,0:T(8,128)S(1)}, u32[]{:S(2)}, u32[]{:S(2)}) collective-permute-start(f32[1,16,128]{2,1,0:T(8,128)S(1)} %get-tuple-element.83), channel_id=1, source_target_pairs={{0,16},{16,32},{32,48},{48,64},{64,80},{80,96},{96,112},{112,128},... | collective-permute-start | bytes 24584 | tf_op jit(solution)/shard_map/ppermute | solution.py:27
  527.2 10.3 %collective-permute-start.38 = (f32[18,1,128]{2,1,0:T(1,128)}, f32[18,1,128]{2,1,0:T(1,128)}, u32[]{:S(2)}, u32[]{:S(2)}) collective-permute-start(f32[18,1,128]{2,1,0:T(1,128)} %get-tuple-element.68), channel_id=1, source_target_pairs={{4,0},{8,4},{12,8},{5,1},{9,5},{13,9},{6,2},{10,6},{14,10},{7,3},{... | collective-permute-start | bytes 27656 | tf_op jit(solution)/shard_map/ppermute | solution.py:28
  528.5 9.0 %collective-permute-start.39 = (f32[18,1,128]{2,1,0:T(1,128)}, f32[18,1,128]{2,1,0:T(1,128)}, u32[]{:S(2)}, u32[]{:S(2)}) collective-permute-start(f32[18,1,128]{2,1,0:T(1,128)} %get-tuple-element.67), channel_id=1, source_target_pairs={{0,4},{4,8},{8,12},{1,5},{5,9},{9,13},{2,6},{6,10},{10,14},{3,7},{... | collective-permute-start | bytes 27656 | tf_op jit(solution)/shard_map/ppermute | solution.py:27
  538.5 25.0 %copy-start.38 = (f32[128,64]{0,1:T(8,128)S(1)}, f32[128,64]{0,1:T(8,128)}, u32[]{:S(2)}) copy-start(f32[128,64]{0,1:T(8,128)} %get-tuple-element.32) | copy-start | bytes 98308
  538.6 5.7 collective-permute-start.41
  541.5 28.1 %copy-start.17 = (f32[64,128]{1,0:T(8,128)S(1)}, f32[64,128]{1,0:T(8,128)}, u32[]{:S(2)}) copy-start(f32[64,128]{1,0:T(8,128)} %get-tuple-element.39) | copy-start | bytes 98308
  541.5 28.1 %copy-start.24 = (f32[64,128]{1,0:T(8,128)S(1)}, f32[64,128]{1,0:T(8,128)}, u32[]{:S(2)}) copy-start(f32[64,128]{1,0:T(8,128)} %get-tuple-element.40) | copy-start | bytes 98308
  541.5 28.1 %copy-start.27 = (f32[64,128]{1,0:T(8,128)S(1)}, f32[64,128]{1,0:T(8,128)}, u32[]{:S(2)}) copy-start(f32[64,128]{1,0:T(8,128)} %get-tuple-element.36) | copy-start | bytes 98308
  541.5 28.1 %copy-start.29 = (bf16[64,128]{1,0:T(8,128)(2,1)S(1)}, bf16[64,128]{1,0:T(8,128)(2,1)}, u32[]{:S(2)}) copy-start(bf16[64,128]{1,0:T(8,128)(2,1)} %copy-done.28) | copy-start | bytes 49156
  541.5 6.8 %collective-permute-start.40 = (f32[18,18,1]{2,1,0:T(8,128)S(1)}, f32[18,18,1]{2,1,0:T(8,128)S(1)}, u32[]{:S(2)}, u32[]{:S(2)}) collective-permute-start(f32[18,18,1]{2,1,0:T(8,128)S(1)} %get-tuple-element.51), channel_id=1, source_target_pairs={{1,0},{2,1},{3,2},{5,4},{6,5},{7,6},{9,8},{10,9},{11,10},{13,12},{... | collective-permute-start | bytes 3896 | tf_op jit(solution)/shard_map/ppermute | solution.py:28
  549.4 14.5 %collective-permute-start.42 = (f32[1,16,128]{2,1,0:T(8,128)S(1)}, f32[1,16,128]{2,1,0:T(8,128)S(1)}, u32[]{:S(2)}, u32[]{:S(2)}) collective-permute-start(f32[1,16,128]{2,1,0:T(8,128)S(1)} %get-tuple-element.82), channel_id=1, source_target_pairs={{16,0},{32,16},{48,32},{64,48},{80,64},{96,80},{112,96},{128,112},... | collective-permute-start | bytes 24584 | tf_op jit(solution)/shard_map/ppermute | solution.py:28
  551.3 13.0 %collective-permute-start.43 = (f32[1,16,128]{2,1,0:T(8,128)S(1)}, f32[1,16,128]{2,1,0:T(8,128)S(1)}, u32[]{:S(2)}, u32[]{:S(2)}) collective-permute-start(f32[1,16,128]{2,1,0:T(8,128)S(1)} %get-tuple-element.81), channel_id=1, source_target_pairs={{0,16},{16,32},{32,48},{48,64},{64,80},{80,96},{96,112},{112,128},... | collective-permute-start | bytes 24584 | tf_op jit(solution)/shard_map/ppermute | solution.py:27
  564.3 6.0 %collective-permute-start.44 = (f32[18,1,128]{2,1,0:T(1,128)S(1)}, f32[18,1,128]{2,1,0:T(1,128)S(1)}, u32[]{:S(2)}, u32[]{:S(2)}) collective-permute-start(f32[18,1,128]{2,1,0:T(1,128)S(1)} %get-tuple-element.66), channel_id=1, source_target_pairs={{4,0},{8,4},{12,8},{5,1},{9,5},{13,9},{6,2},{10,6},{14,10},{7,3},{... | collective-permute-start | bytes 27656 | tf_op jit(solution)/shard_map/ppermute | solution.py:28
  565.6 4.8 collective-permute-start.45
  570.5 6.0 %collective-permute-start.47 = (f32[18,18,1]{2,1,0:T(8,128)S(1)}, f32[18,18,1]{2,1,0:T(8,128)S(1)}, u32[]{:S(2)}, u32[]{:S(2)}) collective-permute-start(f32[18,18,1]{2,1,0:T(8,128)S(1)} %get-tuple-element.50), channel_id=1, source_target_pairs={{0,1},{1,2},{2,3},{4,5},{5,6},{6,7},{8,9},{9,10},{10,11},{12,13},{... | collective-permute-start | bytes 3896 | tf_op jit(solution)/shard_map/ppermute | solution.py:27
  573.7 6.7 %collective-permute-start.46 = (f32[18,18,1]{2,1,0:T(8,128)S(1)}, f32[18,18,1]{2,1,0:T(8,128)S(1)}, u32[]{:S(2)}, u32[]{:S(2)}) collective-permute-start(f32[18,18,1]{2,1,0:T(8,128)S(1)} %get-tuple-element.49), channel_id=1, source_target_pairs={{1,0},{2,1},{3,2},{5,4},{6,5},{7,6},{9,8},{10,9},{11,10},{13,12},{... | collective-permute-start | bytes 3896 | tf_op jit(solution)/shard_map/ppermute | solution.py:28
  (48 other events, 549.8 us)
Sparse Core Ops, SparseCore 0:
  74.2 110.8 reduce-scatter.2
  370.4 102.9 reduce-scatter.4
where the time goes:
time: 596 us; the launch traced here: 588 us
  waiting for transfers between devices  211 us (35%)
  starting transfers between devices  174 us (29%)
  blocking collectives  102 us (17%)
  other arithmetic  45.8 us (8%)
  local copies, waits for them, and re-layouts  39.7 us (7%)
  between operations  15.4 us (3%)
    reduce_scatter x2, waiting for transfers between devices, per_device(): lax.psum_scatter(spread, 'wide', scatter_dimension=1, tiled=True)  183 us
    ppermute x24, starting transfers between devices, padded_2(): before = lax.ppermute(last, axis, up)  133 us
    all_gather x2, blocking collectives, per_device(): table = lax.all_gather(columns, 'wide', axis=1, tiled=True)  102 us
    ppermute x24, starting transfers between devices, padded_2(): after = lax.ppermute(leading, axis, down)  41.1 us
    ppermute x24, waiting for transfers between devices, padded_2(): after = lax.ppermute(leading, axis, down)  24 us
    unnamed x132, local copies, waits for them, and re-layouts  12.8 us
  transfers between devices with their start and end apart: 50, of which 15 were waited for; matrix products, arithmetic and copies ran while one was open for 10% of the time, Pallas kernels for 0%

commit v1 on v0

v1 whole, which is shorter than its diff:
```python
import functools

import jax
import jax.numpy as jnp
from jax import lax
from jax.experimental import pallas as pl
from jax.experimental.pallas import tpu as pltpu
from jax.sharding import PartitionSpec as P

BLOCK = 64
ITERS = 2
SWEEPS = 4
INNER = 2
WIDTH = 4
FAR_FIRST = (2, 1, 3)

CONDUCT = 1.0
COOLING = 0.5
TAIT_C = 0.3
EXPAND = 0.25
BULK_BASE = 0.5
BULK_SLOPE = 0.3

MESH = pl.DeviceIdType.MESH
F32 = jnp.float32
BF16 = jnp.bfloat16


def flip(v, k):
    if k == 0:
        return v
    if k == 1:
        return v + 1 - 2 * (v % 2)
    if k == 2:
        return (v + 2) % 4
    return 3 - v


def split_terms(x):
    hi = x.astype(BF16)
    lo = (x - hi.astype(F32)).astype(BF16)
    return hi, lo


def kernel(
    mold, cap, melt_in, logp, target_in, inflow_in, coef_in, columns_in, owner_in, slot_in, self_in, link_in,
    out_field, out_press, out_shrink,
    selfb, linkb, tab, spread, rs1, psum, rs2, near, rows_in, pack, pack_in, ext, inv, base, plain,
    srcb, src_in, lower, lower_in,
    hot, hot_t, col_hot, diag, kv, resid, jdiag, slope, upd, state, melt, target, inflow, coef,
    columns, owner, slot,
    load_sem, zsend_sem, zrecv_sem, gsend_sem, grecv_sem, csend_sem, crecv_sem, ysend_sem, yrecv_sem,
    xsend_sem, xrecv_sem, lsend_sem, lrecv_sem, wsend_sem, wrecv_sem, msend_sem, mrecv_sem, nsend_sem, nrecv_sem,
):
    cx, cy, cz = mold.shape
    planes, width = near.shape[1], WIDTH
    w = lax.axis_index("wide")
    m = lax.axis_index("mid")
    n = lax.axis_index("narrow")
    n_w, n_m, n_n = lax.axis_size("wide"), lax.axis_size("mid"), lax.axis_size("narrow")
    zh, x, c = w // 8, (w // 2) % 4, w % 2

    def z_peer(k):
        return (flip(zh, k) * 8 + x * 2 + c, m, n)

    def xc_peer(j):
        return (zh * 8 + flip(x, j // 2) * 2 + flip(c, j % 2), m, n)

    def beside(dw, dm, dn):
        return ((w + n_w + dw) % n_w, (m + n_m + dm) % n_m, (n + n_n + dn) % n_n)

    barrier = pltpu.get_barrier_semaphore()
    peers = [z_peer(k) for k in range(1, 4)] + [xc_peer(j) for j in range(1, 8)]
    peers += [beside(-1, 0, 0), beside(1, 0, 0)]
    peers += [beside(0, dm, dn) for dm in (-1, 0, 1) for dn in (-1, 0, 1) if (dm, dn) != (0, 0)]
    for peer in peers:
        pl.semaphore_signal(barrier, inc=1, device_id=peer, device_id_type=MESH)

    loads = [
        pltpu.make_async_copy(src, dst, load_sem.at[i])
        for i, (src, dst) in enumerate((
            (mold, near.at[0, pl.ds(width, cx)]), (cap, near.at[2, pl.ds(width, cx)]),
            (owner_in, owner), (slot_in, slot), (melt_in, melt), (coef_in, coef), (columns_in, columns),
            (self_in, selfb), (link_in, linkb), (logp, state), (target_in, target), (inflow_in, inflow),
        ))
    ]
    for load in loads:
        load.start()

    def remote(src, dst, sems, peer):
        return pltpu.make_async_remote_copy(
            src_ref=src, dst_ref=dst, send_sem=sems[0], recv_sem=sems[1],
            device_id=peer, device_id_type=MESH,
        )

    def w_sems(a, q):
        return (wsend_sem.at[a, q], wrecv_sem.at[a, q])

    def send_low(a):
        remote(
            near.at[a, pl.ds(width, width)], near.at[a, pl.ds(width + cx, width)], w_sems(a, 0), beside(-1, 0, 0)
        ).start()

    def send_high(a):
        remote(near.at[a, pl.ds(cx, width)], near.at[a, pl.ds(0, width)], w_sems(a, 1), beside(1, 0, 0)).start()

    def wide_to_mid(a):
        got = near.at[a, pl.ds(width + cx, width)]
        remote(got, got, w_sems(a, 0), beside(-1, 0, 0)).wait_recv()
        got = near.at[a, pl.ds(0, width)]
        remote(got, got, w_sems(a, 1), beside(1, 0, 0)).wait_recv()
        sems = (msend_sem.at[a], mrecv_sem.at[a])
        remote(near.at[a, :, pl.ds(0, 8)], rows_in.at[a, 0], sems, beside(0, -1, 0)).start()
        remote(near.at[a, :, pl.ds(8, 8)], rows_in.at[a, 1], sems, beside(0, 1, 0)).start()

    lane = lax.broadcasted_iota(jnp.int32, (24, cz), 1)
    row8 = lax.broadcasted_iota(jnp.int32, (8, cz), 0)
    lane8 = lax.broadcasted_iota(jnp.int32, (8, cz), 1)

    def mid_to_narrow(a, dst):
        got = rows_in.at[a]
        remote(got, got, (msend_sem.at[a], mrecv_sem.at[a]), beside(0, 1, 0)).wait_recv()
        packed = [jnp.zeros((24, cz), F32), jnp.zeros((24, cz), F32)]
        for p in range(planes):
            ghost = jnp.where(row8 < width, rows_in[a, 0, p], rows_in[a, 1, p])
            whole = jnp.concatenate([near[a, p], ghost], axis=0)
            dst[p, :, 0:cz] = whole
            g, q = p // 16, p % 16
            packed[g] = jnp.where(lane // 8 == q, pltpu.roll(whole, width + 8 * q, 1), packed[g])
        for g in range(2):
            pack[a, g] = packed[g]
        sems = (nsend_sem.at[a], nrecv_sem.at[a])
        remote(pack.at[a], pack_in.at[a, 0], sems, beside(0, 0, -1)).start()
        remote(pack.at[a], pack_in.at[a, 1], sems, beside(0, 0, 1)).start()

    def narrow_done(a, dst):
        got = pack_in.at[a]
        remote(got, got, (nsend_sem.at[a], nrecv_sem.at[a]), beside(0, 0, 1)).wait_recv()
        for g in range(2):
            comb = jnp.where(lane % 8 >= width, pack_in[a, 0, g], pack_in[a, 1, g])
            for p in range(16 * g, min(planes, 16 * g + 16)):
                dst[p, :, cz:2 * cz] = pltpu.roll(comb, cz - (8 * (p % 16) + width), 1)

    row_at = lax.broadcasted_iota(jnp.int32, (24, 2 * cz), 0)
    row_at = jnp.where(row_at < cy + width, row_at, row_at - 24) + m * cy
    lane_at = lax.broadcasted_iota(jnp.int32, (24, 2 * cz), 1)
    lane_real = (lane_at < cz + width) | (lane_at >= 2 * cz - width)
    lane_at = jnp.where(lane_at < cz + width, lane_at, lane_at - 2 * cz) + n * cz
    inside = lane_real & (row_at >= 0) & (row_at < n_m * cy) & (lane_at >= 0) & (lane_at < n_n * cz)
    inside = jnp.where(inside, 1.0, 0.0)

    def prepare():
        for p in range(planes):
            here = inside
            if p < width:
                here = jnp.where(w > 0, inside, 0.0)
            elif p >= width + cx:
                here = jnp.where(w < n_w - 1, inside, 0.0)
            capacity, start = inv[p], ext[0, p]
            base[p] = capacity * start
            inv[p] = here / (capacity + 6.0 * CONDUCT)
            ext[0, p] = jnp.where(here > 0.0, start, 0.0)

    def around(plane):
        rows = pltpu.roll(plane, 1, 0) + pltpu.roll(plane, 23, 0)
        return rows + (pltpu.roll(plane, 1, 1) + pltpu.roll(plane, 2 * cz - 1, 1))

    def plain_sweeps():
        for k in range(SWEEPS):
            now, later = k % 2, (k + 1) % 2
            edge = k + 1
            for p in range(edge, planes - edge):
                total = (ext[now, p - 1] + ext[now, p + 1]) + around(ext[now, p]) + base[p]
                new = total * inv[p]
                if k == SWEEPS - 1:
                    plain[p - width] = new[:cy, :cz]
                else:
                    ext[later, p] = new

    def apply(v16):
        v = v16.astype(F32)
        linked = jnp.dot(v16, col_hot[...], preferred_element_type=F32)
        near0, near1 = linked[:, :128], linked[:, 128:]

        def rows(t, carry):
            sums = []
            for u in range(8):
                i = t * 8 + u
                prod = selfb[i].astype(F32) * v + linkb[0, i].astype(F32) * near0 + linkb[1, i].astype(F32) * near1
                sums.append(jnp.sum(prod, axis=0, keepdims=True))
            kv[pl.ds(pl.multiple_of(t * 8, 8), 8), :] = jnp.concatenate(sums, axis=0)
            return carry

        lax.fori_loop(0, BLOCK // 8, rows, 0)
        return kv[...]

    def newton_start():
        mt, st = melt[...], state[...]
        bulk = BULK_BASE * jnp.exp(-BULK_SLOPE * mt)
        growth = jnp.exp(st)
        press = bulk * (growth - 1.0)
        base_volume = jnp.exp(EXPAND * mt)
        volume = base_volume * (1.0 - TAIT_C * st)
        sl = bulk * growth
        slope[...] = sl
        jd = diag[...] * sl + TAIT_C * base_volume
        jdiag[...] = jd
        res = apply(press.astype(BF16)) + (target[...] - volume) - inflow[...]
        resid[...] = res
        upd[...] = -res / jd

    def newton_step():
        weighted = (slope[...] * upd[...]).astype(BF16)
        linked = apply(weighted) - diag[...] * weighted.astype(F32)
        upd[...] = (-resid[...] - linked) / jdiag[...]

    def gather_start(it):
        for k in FAR_FIRST:
            remote(tab.at[it, 0, 0], tab.at[it, k, 0], z_sems(it, k), z_peer(k)).start()
        gather_on(it, 0)

    def z_sems(it, k):
        return (zsend_sem.at[it, k], zrecv_sem.at[it, k])

    def gather_sems(it, k):
        return (gsend_sem.at[it, k], grecv_sem.at[it, k])

    def scatter_sems(it, k):
        return (csend_sem.at[it, k], crecv_sem.at[it, k])

    def sum_sems(it, k):
        return (ysend_sem.at[it, k], yrecv_sem.at[it, k])

    def gather_on(it, k):
        for j in range(1, 8):
            remote(tab.at[it, k, 0], tab.at[it, k, j], gather_sems(it, k), xc_peer(j)).start()

    def z_arrived(it, k):
        got = tab.at[it, k, 0]
        remote(got, got, z_sems(it, k), z_peer(k)).wait_recv()
        gather_on(it, k)

    for it in range(ITERS):
        src_in[it] = jnp.zeros((10, 8, cz), F32)
    loads[0].wait()
    tab[0, 0, 0] = near[0, width]
    pl.semaphore_wait(barrier, len(peers))
    gather_start(0)
    send_low(0)
    send_high(0)
    loads[1].wait()
    send_low(2)
    send_high(2)

    for it in range(ITERS):
        if it == 0:
            loads[2].wait()
            loads[3].wait()
            rel = jnp.bitwise_xor(owner[...], w)
            place = rel * 16 + slot[...] // 2
            half = slot[...] % 2
            faces = lax.broadcasted_iota(jnp.int32, (512, 128), 0)
            hot32 = jnp.where(faces == place, 1.0, 0.0)
            hot[...] = hot32.astype(BF16)
            hot_t[...] = hot32.T.astype(BF16)
        z_arrived(it, 1)
        z_arrived(it, 3)
        z_arrived(it, 2)
        if it == 0:
            for load in loads[4:]:
                load.wait()
            froms = lax.broadcasted_iota(jnp.int32, (128, 128), 0)
            for k in range(2):
                col_hot[:, k * 128:(k + 1) * 128] = jnp.where(froms == columns[k:k + 1, :], 1.0, 0.0).astype(BF16)
            wide_to_mid(0)
            wide_to_mid(2)

            def pick(t, carry):
                sums = []
                for u in range(8):
                    i = t * 8 + u
                    mask = lax.broadcasted_iota(jnp.int32, (BLOCK, 128), 0) == i
                    sums.append(jnp.sum(jnp.where(mask, selfb[i].astype(F32), 0.0), axis=0, keepdims=True))
                diag[pl.ds(pl.multiple_of(t * 8, 8), 8), :] = jnp.concatenate(sums, axis=0)
                return carry

            lax.fori_loop(0, BLOCK // 8, pick, 0)
        else:
            got = lower_in.at[it - 1]
            remote(got, got, (lsend_sem.at[it - 1], lrecv_sem.at[it - 1]), beside(1, 0, 0)).wait_recv()
            for p in range(3):
                near[1, width + cx - 3 + p] = plain[cx - 3 + p] + lower_in[it - 1, p]
            send_high(1)
            for p in range(width, cx - width):
                near[1, width + p] = plain[p]
        found = jnp.zeros((128, 256), F32)
        for k in (0, 1, 3, 2):
            got = tab.at[it, k, pl.ds(1, 7)]
            remote(got, got, gather_sems(it, k), xc_peer(1)).wait_recv()
            hi, lo = split_terms(tab[it, k].reshape(128, 128))
            found = found + jnp.dot(
                hot_t[:, k * 128:(k + 1) * 128], jnp.concatenate([hi, lo], axis=1), preferred_element_type=F32
            )
        found = (found[:, :128] + found[:, 128:]).T
        wall = jnp.where(half == 1, found[BLOCK:], found[:BLOCK])
        flux = coef[...] * (melt[...] - wall)
        melt[...] = melt[...] - COOLING * flux
        placed = jnp.concatenate([jnp.where(half == 0, flux, 0.0), jnp.where(half == 1, flux, 0.0)], axis=0)
        hi, lo = split_terms(placed)
        terms = jnp.concatenate([hi, lo], axis=0)
        for k in FAR_FIRST + (0,):
            summed = lax.dot_general(
                hot[k * 128:(k + 1) * 128, :], terms, (((1,), (1,)), ((), ())), preferred_element_type=F32
            )
            spread[it, k] = (summed[:, :128] + summed[:, 128:]).reshape(8, 16, 128)
            for j in range(1, 8):
                remote(spread.at[it, k, j], rs1.at[it, k, j], scatter_sems(it, k), xc_peer(j)).start()
        if it > 0:
            wide_to_mid(1)
        newton_start()
        for k in FAR_FIRST + (0,):
            got = rs1.at[it, k, pl.ds(1, 7)]
            remote(got, got, scatter_sems(it, k), xc_peer(1)).wait_recv()
            total = spread[it, k, 0]
            for j in range(1, 8):
                total = total + rs1[it, k, j]
            psum[it, k] = total
            if k > 0:
                remote(psum.at[it, k], rs2.at[it, k], sum_sems(it, k), z_peer(k)).start()
        if it == 0:
            mid_to_narrow(0, ext.at[0])
            mid_to_narrow(2, inv)
            newton_step()
            narrow_done(0, ext.at[0])
            narrow_done(2, inv)
            prepare()
        else:
            mid_to_narrow(1, ext.at[0])
            newton_step()
            narrow_done(1, ext.at[0])
            for p in range(planes):
                ext[0, p] = jnp.where(inv[p] > 0.0, ext[0, p], 0.0)
        plain_sweeps()
        source = psum[it, 0]
        for k in (1, 3, 2):
            got = rs2.at[it, k]
            remote(got, got, sum_sems(it, k), z_peer(k)).wait_recv()
            source = source + rs2[it, k]
        srcb[it, 0] = source[:8]
        srcb[it, 1] = source[8:]
        def send_edges(side, parts):
            for src, place_at, count, dm, dn in parts:
                remote(
                    srcb.at[it, pl.ds(src, count)], src_in.at[it, pl.ds(place_at, count)],
                    (xsend_sem.at[it, side], xrecv_sem.at[it, side]), beside(0, dm, dn),
                ).start()

        send_edges(0, ((0, 0, 1, -1, 0), (1, 1, 1, 1, 0)))

        @pl.when(n > 0)
        def _():
            send_edges(1, ((0, 2, 2, 0, -1), (0, 4, 1, -1, -1), (1, 5, 1, 1, -1)))

        @pl.when(n < n_n - 1)
        def _():
            send_edges(2, ((0, 6, 2, 0, 1), (0, 8, 1, -1, 1), (1, 9, 1, 1, 1)))

        newton_step()
        state[...] = state[...] + upd[...]
        if it == ITERS - 1:
            mt, st = melt[...], state[...]
            out_press[...] = BULK_BASE * jnp.exp(-BULK_SLOPE * mt) * (jnp.exp(st) - 1.0)
            out_shrink[...] = 1.0 - jnp.exp(EXPAND * mt) * (1.0 - TAIT_C * st)
        def edges(side, first, count):
            got = src_in.at[it, pl.ds(first, count)]
            return remote(got, got, (xsend_sem.at[it, side], xrecv_sem.at[it, side]), beside(0, 1, 0))

        edges(0, 0, 2).wait_recv()

        @pl.when(n < n_n - 1)
        def _():
            edges(1, 2, 4).wait_recv()

        @pl.when(n > 0)
        def _():
            edges(2, 6, 4).wait_recv()

        def corner(up, down):
            return jnp.where(row8 < width, src_in[it, up], src_in[it, down])

        def lanes(after, before):
            return jnp.where(lane8 < width, after, before)

        main = jnp.concatenate([source, corner(0, 1)], axis=0)
        sides = jnp.concatenate(
            [lanes(src_in[it, 2], src_in[it, 6]), lanes(src_in[it, 3], src_in[it, 7]), lanes(corner(4, 5), corner(8, 9))],
            axis=0,
        )
        wide_source = jnp.concatenate([main, sides], axis=1)
        nothing = jnp.zeros((24, 2 * cz), F32)
        level = [{0: wide_source * inv[width]}]

        def grown(k, p):
            have = level[k - 1]
            total = nothing
            if p == 0:
                total = wide_source
            for q in (p - 1, p + 1):
                if q in have:
                    total = total + have[q]
            if p in have:
                total = total + around(have[p])
            return total * inv[width + p]

        level.append({p: grown(1, p) for p in (0, -1, 1)})
        level.append({p: grown(2, p) for p in (0, -1, 1)})
        wall_plane = plain[0] + grown(3, 0)[:cy, :cz]
        if it < ITERS - 1:
            tab[it + 1, 0, 0] = wall_plane
            gather_start(it + 1)
        level[2].update({p: grown(2, p) for p in (-2, 2)})
        for p in (-3, -2, -1):
            lower[it, p + 3] = grown(3, p)[:cy, :cz]
        remote(lower.at[it], lower_in.at[it], (lsend_sem.at[it], lrecv_sem.at[it]), beside(-1, 0, 0)).start()
        first = [wall_plane] + [plain[p] + grown(3, p)[:cy, :cz] for p in (1, 2, 3)]
        if it < ITERS - 1:
            for p in range(4):
                near[1, width + p] = first[p]
            send_low(1)
            near[1, cx] = plain[cx - 4]
        else:
            for p in range(4):
                out_field[p] = first[p]
            for p in range(4, cx - 3):
                out_field[p] = plain[p]
            got = lower_in.at[it]
            remote(got, got, (lsend_sem.at[it], lrecv_sem.at[it]), beside(1, 0, 0)).wait_recv()
            for p in range(3):
                out_field[cx - 3 + p] = plain[cx - 3 + p] + lower_in[it, p]

    for it in range(ITERS):
        for k in range(4):
            if k > 0:
                remote(tab.at[it, k, 0], tab.at[it, k, 0], z_sems(it, k), z_peer(k)).wait_send()
                remote(psum.at[it, k], psum.at[it, k], sum_sems(it, k), z_peer(k)).wait_send()
            region = tab.at[it, k, pl.ds(1, 7)]
            remote(region, region, gather_sems(it, k), z_peer(1)).wait_send()
            region = spread.at[it, k, pl.ds(1, 7)]
            remote(region, region, scatter_sems(it, k), z_peer(1)).wait_send()
        for side, first, count, sent in ((0, 0, 2, None), (1, 2, 4, n > 0), (2, 6, 4, n < n_n - 1)):
            region = src_in.at[it, pl.ds(first, count)]
            edge = remote(region, region, (xsend_sem.at[it, side], xrecv_sem.at[it, side]), z_peer(1))
            if sent is None:
                edge.wait_send()
            else:
                pl.when(sent)(edge.wait_send)
        remote(lower.at[it], lower.at[it], (lsend_sem.at[it], lrecv_sem.at[it]), z_peer(1)).wait_send()
    for a in range(3):
        for q in range(2):
            region = near.at[a, pl.ds(0, width)]
            remote(region, region, w_sems(a, q), z_peer(1)).wait_send()
        region = rows_in.at[a]
        remote(region, region, (msend_sem.at[a], mrecv_sem.at[a]), z_peer(1)).wait_send()
        region = pack_in.at[a]
        remote(region, region, (nsend_sem.at[a], nrecv_sem.at[a]), z_peer(1)).wait_send()


def per_device(
    mold_temp, capacity, melt_temp, log_pressure, target_volume, inflow, self_blocks, link_blocks,
    link_columns, wall_owner, wall_slot, transfer_coef,
):
    cx, cy, cz = mold_temp.shape
    cells, blocks = melt_temp.shape
    planes = cx + 2 * WIDTH
    vmem = pl.BlockSpec(memory_space=pltpu.VMEM)
    hbm = pl.BlockSpec(memory_space=pltpu.HBM)

    def scratch(*shape):
        return pltpu.VMEM(shape, F32)

    cav = scratch(cells, blocks)
    return pl.pallas_call(
        kernel,
        out_shape=(
            jax.ShapeDtypeStruct(mold_temp.shape, F32),
            jax.ShapeDtypeStruct(melt_temp.shape, F32),
            jax.ShapeDtypeStruct(melt_temp.shape, F32),
        ),
        in_specs=[hbm] * 12,
        out_specs=(vmem, vmem, vmem),
        scratch_shapes=[
            pltpu.VMEM(self_blocks.shape, BF16),
            pltpu.VMEM(link_blocks.shape, BF16),
            scratch(ITERS, 4, 8, 16, 128),
            scratch(ITERS, 4, 8, 16, 128),
            scratch(ITERS, 4, 8, 16, 128),
            scratch(ITERS, 4, 16, 128),
            scratch(ITERS, 4, 16, 128),
            scratch(3, planes, cy, cz),
            scratch(3, 2, planes, 8, cz),
            scratch(3, 2, 24, cz),
            scratch(3, 2, 2, 24, cz),
            scratch(2, planes, 24, 2 * cz),
            scratch(planes, 24, 2 * cz),
            scratch(planes, 24, 2 * cz),
            scratch(cx, cy, cz),
            scratch(ITERS, 2, 8, cz),
            scratch(ITERS, 10, 8, cz),
            scratch(ITERS, 3, cy, cz),
            scratch(ITERS, 3, cy, cz),
            pltpu.VMEM((512, 128), BF16),
            pltpu.VMEM((128, 512), BF16),
            pltpu.VMEM((128, 256), BF16),
            cav, cav, cav, cav, cav, cav, cav, cav, cav, cav, cav,
            pltpu.VMEM((2, blocks), jnp.int32),
            pltpu.VMEM((1, blocks), jnp.int32),
            pltpu.VMEM((1, blocks), jnp.int32),
            pltpu.SemaphoreType.DMA((12,)),
            *[pltpu.SemaphoreType.DMA((ITERS, 4))] * 8,
            *[pltpu.SemaphoreType.DMA((ITERS, 3))] * 2,
            *[pltpu.SemaphoreType.DMA((ITERS,))] * 2,
            pltpu.SemaphoreType.DMA((3, 2)),
            pltpu.SemaphoreType.DMA((3, 2)),
            pltpu.SemaphoreType.DMA((3,)),
            pltpu.SemaphoreType.DMA((3,)),
            pltpu.SemaphoreType.DMA((3,)),
            pltpu.SemaphoreType.DMA((3,)),
        ],
        compiler_params=pltpu.CompilerParams(
            collective_id=0, has_side_effects=True, vmem_limit_bytes=56 * 1024 * 1024
        ),
    )(
        mold_temp, capacity, melt_temp, log_pressure, target_volume, inflow, transfer_coef,
        link_columns, wall_owner.reshape(1, blocks), wall_slot.reshape(1, blocks), self_blocks, link_blocks,
    )


def solution(mesh):
    cavity = P(None, ("wide", "mid", "narrow"))
    brick = P("wide", "mid", "narrow")
    flat = P(("wide", "mid", "narrow"))
    return jax.shard_map(
        per_device,
        mesh=mesh,
        in_specs=(
            brick, brick, cavity, cavity, cavity, cavity,
            P(None, None, ("wide", "mid", "narrow")),
            P(None, None, None, ("wide", "mid", "narrow")),
            cavity, flat, flat, cavity,
        ),
        out_specs=(brick, cavity, cavity),
        check_vma=False,
    )
```

time: 596 us -> 81.5 us (0.14); the launches traced: 588 us -> 81.2 us
  waiting for transfers between devices: 211 us -> 0 us
  starting transfers between devices: 174 us -> 0 us
  blocking collectives: 102 us -> 0 us
  Pallas kernels: 0 us -> 76.3 us
  other arithmetic: 45.8 us -> 0 us
  local copies, waits for them, and re-layouts: 39.7 us -> 4.32 us
  between operations: 15.4 us -> 0.64 us
    reduce_scatter x2 -> x0, waiting for transfers between devices: 183 us -> none  [per_device(): lax.psum_scatter(spread, 'wide', scatter_dimension=1, tiled=True)]
    ppermute x48 -> x0, starting transfers between devices: 174 us -> none  [the longest x24 133 us: padded_2(): before = lax.ppermute(last, axis, up)]
    all_gather x2 -> x0, blocking collectives: 102 us -> none  [per_device(): table = lax.all_gather(columns, 'wide', axis=1, tiled=True)]
    pallas_call x0 -> x1, Pallas kernels: none -> 76.3 us  [per_device(): pl.pallas_call(kernel, out_shape=(jax.ShapeDtypeStruct(mold_temp.shape, F...]
    ppermute x48 -> x0, waiting for transfers between devices: 27.7 us -> none  [the longest x24 24 us: padded_2(): after = lax.ppermute(leading, axis, down)]
    dot_general x12 -> x0, other arithmetic: 14.2 us -> none  [the longest x6 10.1 us: block_apply(): jnp.einsum('nijb,jnb->ib', link_blocks, nearby, preferred_element_type=jn...]
    gather x11 -> x0, local copies, waits for them, and re-layouts: 14.1 us -> none  [the longest x6 10.1 us: block_apply(): nearby = values[:, link_columns]]
    div x8 -> x0, other arithmetic: 9.48 us -> none  [per_device(): (capacity * mold_temp + source + CONDUCT * beside_of(padded)) / (capacity...]
  transfers between devices with their start and end apart: 50 -> 0, of which waited for: 15 -> 0; matrix products, arithmetic and copies ran while one was open for 10% -> 0% of each run, Pallas kernels for 0% -> 0%
where the time goes in v1:
time: 81.5 us; the launch traced here: 81.2 us
  Pallas kernels  76.3 us (94%)
  local copies, waits for them, and re-layouts  4.32 us (5%)
    pallas_call x1, Pallas kernels, per_device(): pl.pallas_call(kernel, out_shape=(jax.ShapeDtypeStruct(mold_temp.shape, F...  76.3 us
    unnamed x3, local copies, waits for them, and re-layouts  4.32 us

profile of v1, /device:TPU:7, one launch (start us, length us, event | category | flops | bytes accessed | tf_op | source)
XLA Modules:
  0.0 81.2 jit_solution(15164398463914218170)
XLA Ops:
  0.6 76.3 %shard_map.139 = (f32[16,16,128]{2,1,0:T(8,128)}, f32[64,128]{1,0:T(8,128)}, f32[64,128]{1,0:T(8,128)}) custom-call(f32[16,16,128]{2,1,0:T(8,128)} %mold.1, f32[16,16,128]{2,1,0:T(8,128)} %cap.1, f32[64,128]{1,0:T(8,128)} %melt_in.1, f32[64,128]{1,0:T(8,128)} %logp.1, f32[64,128]{1,0:T(8,128)} %target_in.1, f32[64,128]{1,0:T(8,128)} %inflow_in.1, ...), custom_call_target="tpu_custom_call" | custom-call | tf_op jit(solution)/shard_map/pallas_call | solution.py:482
  76.9 1.6 %copy.18 = f32[16,16,128]{2,1,0:T(8,128)} copy(f32[16,16,128]{2,1,0:T(8,128)} %get-tuple-element.6) | data formatting | bytes 262144
  78.5 1.4 %copy.19 = f32[64,128]{1,0:T(8,128)} copy(f32[64,128]{1,0:T(8,128)} %get-tuple-element.7) | data formatting | bytes 65536
  79.9 1.4 %copy.20 = f32[64,128]{1,0:T(8,128)} copy(f32[64,128]{1,0:T(8,128)} %get-tuple-element.8) | data formatting | bytes 65536

commit v2 on v0

v2 whole, which is shorter than its diff:
```python
import functools

import jax
import jax.numpy as jnp
from jax import lax
from jax.experimental import pallas as pl
from jax.experimental.pallas import tpu as pltpu
from jax.sharding import PartitionSpec as P

BLOCK = 64
ITERS = 2
SWEEPS = 4
INNER = 2
WIDTH = 4
FAR_FIRST = (2, 1, 3)

CONDUCT = 1.0
COOLING = 0.5
TAIT_C = 0.3
EXPAND = 0.25
BULK_BASE = 0.5
BULK_SLOPE = 0.3

MESH = pl.DeviceIdType.MESH
F32 = jnp.float32
BF16 = jnp.bfloat16


def flip(v, k):
    if k == 0:
        return v
    if k == 1:
        return v + 1 - 2 * (v % 2)
    if k == 2:
        return (v + 2) % 4
    return 3 - v


def split_terms(x):
    hi = x.astype(BF16)
    lo = (x - hi.astype(F32)).astype(BF16)
    return hi, lo


def kernel(
    mold, cap, melt_in, logp, target_in, inflow_in, coef_in, columns_in, owner_in, slot_in, self_in, link_in,
    out_field, out_press, out_shrink,
    selfb, linkb, tab, spread, rs1, psum, rs2, near,
    row_own, row_ghost, lane_own, lane_ghost, rows_own, rows_ghost, lanes_own, lanes_ghost, corner_own, corner_ghost,
    ext, inv, base, plain, srcb, src_in, lower, lower_in,
    hot, hot_t, col_hot, diag, kv, resid, jdiag, slope, upd, state, melt, target, inflow, coef,
    columns, owner, slot,
    load_sem, zsend_sem, zrecv_sem, gsend_sem, grecv_sem, csend_sem, crecv_sem, ysend_sem, yrecv_sem,
    xsend_sem, xrecv_sem, lsend_sem, lrecv_sem, hsend_sem, hrecv_sem,
):
    cx, cy, cz = mold.shape
    planes = near.shape[1]
    w = lax.axis_index("wide")
    m = lax.axis_index("mid")
    n = lax.axis_index("narrow")
    n_w, n_m, n_n = lax.axis_size("wide"), lax.axis_size("mid"), lax.axis_size("narrow")
    zh, x, c = w // 8, (w // 2) % 4, w % 2

    def z_peer(k):
        return (flip(zh, k) * 8 + x * 2 + c, m, n)

    def xc_peer(j):
        return (zh * 8 + flip(x, j // 2) * 2 + flip(c, j % 2), m, n)

    def beside(dw, dm, dn):
        return ((w + n_w + dw) % n_w, (m + n_m + dm) % n_m, (n + n_n + dn) % n_n)

    barrier = pltpu.get_barrier_semaphore()
    peers = [z_peer(k) for k in range(1, 4)] + [xc_peer(j) for j in range(1, 8)]
    peers += [beside(-1, 0, 0), beside(1, 0, 0)]
    peers += [beside(0, dm, dn) for dm in (-1, 0, 1) for dn in (-1, 0, 1) if (dm, dn) != (0, 0)]
    for peer in peers:
        pl.semaphore_signal(barrier, inc=1, device_id=peer, device_id_type=MESH)

    loads = [
        pltpu.make_async_copy(src, dst, load_sem.at[i])
        for i, (src, dst) in enumerate((
            (owner_in, owner), (slot_in, slot), (coef_in, coef), (melt_in, melt),
            (mold, near.at[0, pl.ds(WIDTH, cx)]), (cap, near.at[1, pl.ds(WIDTH, cx)]), (columns_in, columns),
            (self_in, selfb), (link_in, linkb), (logp, state), (target_in, target), (inflow_in, inflow),
        ))
    ]
    for load in loads:
        load.start()

    def remote(src, dst, sems, peer):
        return pltpu.make_async_remote_copy(
            src_ref=src, dst_ref=dst, send_sem=sems[0], recv_sem=sems[1],
            device_id=peer, device_id_type=MESH,
        )

    def wait_recv(region, sems):
        remote(region, region, sems, beside(0, 1, 0)).wait_recv()

    def z_sems(it, k):
        return (zsend_sem.at[it, k], zrecv_sem.at[it, k])

    def gather_sems(it, k):
        return (gsend_sem.at[it, k], grecv_sem.at[it, k])

    def gather_on(it, k):
        for j in range(1, 8):
            remote(tab.at[it, k, 0], tab.at[it, k, j], gather_sems(it, k), xc_peer(j)).start()

    def gather_start(it):
        for k in FAR_FIRST:
            remote(tab.at[it, 0, 0], tab.at[it, k, 0], z_sems(it, k), z_peer(k)).start()

    def z_arrived(it, k):
        wait_recv(tab.at[it, k, 0], z_sems(it, k))
        gather_on(it, k)

    def cool(it):
        found = jnp.zeros((128, 256), F32)
        for k in (0, 1, 3, 2):
            wait_recv(tab.at[it, k, pl.ds(1, 7)], gather_sems(it, k))
            hi, lo = split_terms(tab[it, k].reshape(128, 128))
            found = found + jnp.dot(
                hot_t[:, k * 128:(k + 1) * 128], jnp.concatenate([hi, lo], axis=1), preferred_element_type=F32
            )
        found = (found[:, :128] + found[:, 128:]).T
        wall = jnp.where(half == 1, found[BLOCK:], found[:BLOCK])
        melt[...] = melt[...] - COOLING * (coef[...] * (melt[...] - wall))

    def scatter_sems(a, k):
        return (csend_sem.at[a, k], crecv_sem.at[a, k])

    def sum_sems(a, k):
        return (ysend_sem.at[a, k], yrecv_sem.at[a, k])

    def scatter_terms(values):
        parts = []
        for value in values:
            placed = jnp.concatenate([jnp.where(half == 0, value, 0.0), jnp.where(half == 1, value, 0.0)], axis=0)
            parts.extend(split_terms(placed))
        return jnp.concatenate(parts, axis=0)

    def scatter_start(a, terms):
        for k in FAR_FIRST + (0,):
            summed = lax.dot_general(
                hot[k * 128:(k + 1) * 128, :], terms, (((1,), (1,)), ((), ())), preferred_element_type=F32
            )
            for q in range(2):
                one = summed[:, 256 * q:256 * q + 128] + summed[:, 256 * q + 128:256 * q + 256]
                spread[a, k, :, q] = one.reshape(8, 16, 128)
            for j in range(1, 8):
                remote(spread.at[a, k, j], rs1.at[a, k, j], scatter_sems(a, k), xc_peer(j)).start()

    def scatter_on(a, k):
        wait_recv(rs1.at[a, k, pl.ds(1, 7)], scatter_sems(a, k))
        for q in range(2):
            total = spread[a, k, 0, q]
            for j in range(1, 8):
                total = total + rs1[a, k, j, q]
            psum[a, k, q] = total
        if k > 0:
            remote(psum.at[a, k], rs2.at[a, k], sum_sems(a, k), z_peer(k)).start()

    def scatter_done(a):
        for k in (1, 3, 2):
            wait_recv(rs2.at[a, k], sum_sems(a, k))
        return [((psum[a, 0, q] + rs2[a, 1, q]) + (rs2[a, 3, q] + rs2[a, 2, q])) for q in range(2)]

    lane = lax.broadcasted_iota(jnp.int32, (cy, cz), 1)
    lane24 = lax.broadcasted_iota(jnp.int32, (24, cz), 1)
    row8 = lax.broadcasted_iota(jnp.int32, (8, cz), 0)
    lane8 = lax.broadcasted_iota(jnp.int32, (8, cz), 1)
    own_planes = list(range(WIDTH, WIDTH + cx))
    ghost_planes = list(range(WIDTH)) + list(range(WIDTH + cx, planes))
    arrays = ((0, 1), (2,))

    def h_sems(g, step, kind):
        return (hsend_sem.at[g, step, kind], hrecv_sem.at[g, step, kind])

    def group(g):
        return pl.ds(arrays[g][0], len(arrays[g]))

    def send_low(g):
        remote(
            near.at[group(g), pl.ds(WIDTH, WIDTH)], near.at[group(g), pl.ds(WIDTH + cx, WIDTH)],
            h_sems(g, 0, 0), beside(-1, 0, 0),
        ).start()

    def send_high(g):
        remote(
            near.at[group(g), pl.ds(cx, WIDTH)], near.at[group(g), pl.ds(0, WIDTH)], h_sems(g, 0, 1), beside(1, 0, 0)
        ).start()

    def send_edges(g, step):
        which, row_out, lane_out, rows_in, lanes_in, corner_in = (
            (own_planes, row_own, lane_own, rows_own, lanes_own, corner_own),
            (ghost_planes, row_ghost, lane_ghost, rows_ghost, lanes_ghost, corner_ghost),
        )[step]
        for a in arrays[g]:
            packed = jnp.zeros((cy, cz), F32)
            for q, p in enumerate(which):
                packed = jnp.where(lane // 8 == q, pltpu.roll(near[a, p], WIDTH + 8 * q, 1), packed)
            lane_out[a, 0] = packed[:8]
            lane_out[a, 1] = packed[8:]
            for t in range(len(which) // 2):
                q = 4 * (t // 2) + t % 2
                one, two = near[a, which[q]], near[a, which[q + 2]]
                row_out[a, 0, t] = jnp.where(row8 < WIDTH, one[:8], pltpu.roll(two[:8], 4, 0))
                row_out[a, 1, t] = jnp.where(row8 < WIDTH, pltpu.roll(one[8:], 4, 0), two[8:])
        some = group(g)
        for side, dm in ((0, -1), (1, 1)):
            remote(row_out.at[some, side], rows_in.at[some, side], h_sems(g, step, 2), beside(0, dm, 0)).start()
        for side, dn in ((0, -1), (1, 1)):
            remote(lane_out.at[some], lanes_in.at[some, side], h_sems(g, step, 3), beside(0, 0, dn)).start()
            for tile, dm in ((0, -1), (1, 1)):
                remote(
                    lane_out.at[some, tile], corner_in.at[some, side, tile], h_sems(g, step, 4), beside(0, dm, dn)
                ).start()

    def take_edges(g, step, places):
        which, rows_in, lanes_in, corner_in = (
            (own_planes, rows_own, lanes_own, corner_own), (ghost_planes, rows_ghost, lanes_ghost, corner_ghost),
        )[step]
        some = group(g)
        for kind, region in ((2, rows_in), (3, lanes_in), (4, corner_in)):
            wait_recv(region.at[some], h_sems(g, step, kind))
        for a, dst in zip(arrays[g], places):
            sides = []
            for side in range(2):
                corner = jnp.where(row8 < WIDTH, corner_in[a, side, 0], corner_in[a, side, 1])
                sides.append(jnp.concatenate([lanes_in[a, side, 0], lanes_in[a, side, 1], corner], axis=0))
            comb = jnp.where(lane24 % 8 >= WIDTH, sides[0], sides[1])
            for t in range(len(which) // 2):
                q = 4 * (t // 2) + t % 2
                after, before = rows_in[a, 0, t], rows_in[a, 1, t]
                ghosts = (
                    (q, jnp.where(row8 < WIDTH, after, pltpu.roll(before, 4, 0))),
                    (q + 2, jnp.where(row8 < WIDTH, pltpu.roll(after, 4, 0), before)),
                )
                for at, ghost in ghosts:
                    p = which[at]
                    dst[p, 0:cy, 0:cz] = near[a, p]
                    dst[p, cy:24, 0:cz] = ghost
                    dst[p, :, cz:2 * cz] = pltpu.roll(comb, cz - (8 * at + WIDTH), 1)

    def wide_arrived(g):
        wait_recv(near.at[group(g), pl.ds(WIDTH + cx, WIDTH)], h_sems(g, 0, 0))
        wait_recv(near.at[group(g), pl.ds(0, WIDTH)], h_sems(g, 0, 1))
        send_edges(g, 1)

    def prepare():
        row_at = lax.broadcasted_iota(jnp.int32, (24, 2 * cz), 0)
        row_at = jnp.where(row_at < cy + WIDTH, row_at, row_at - 24) + m * cy
        lane_at = lax.broadcasted_iota(jnp.int32, (24, 2 * cz), 1)
        lane_real = (lane_at < cz + WIDTH) | (lane_at >= 2 * cz - WIDTH)
        lane_at = jnp.where(lane_at < cz + WIDTH, lane_at, lane_at - 2 * cz) + n * cz
        inside = lane_real & (row_at >= 0) & (row_at < n_m * cy) & (lane_at >= 0) & (lane_at < n_n * cz)
        inside = jnp.where(inside, 1.0, 0.0)
        for p in range(planes):
            here = inside
            if p < WIDTH:
                here = jnp.where(w > 0, inside, 0.0)
            elif p >= WIDTH + cx:
                here = jnp.where(w < n_w - 1, inside, 0.0)
            capacity, start = inv[p], ext[0, p]
            base[p] = capacity * start
            inv[p] = here / (capacity + 6.0 * CONDUCT)
            ext[0, p] = jnp.where(here > 0.0, start, 0.0)

    def around(plane):
        rows = pltpu.roll(plane, 1, 0) + pltpu.roll(plane, 23, 0)
        return rows + (pltpu.roll(plane, 1, 1) + pltpu.roll(plane, 2 * cz - 1, 1))

    def plain_sweeps():
        for k in range(SWEEPS):
            now, later = k % 2, (k + 1) % 2
            edge = k + 1
            for p in range(edge, planes - edge):
                total = (ext[now, p - 1] + ext[now, p + 1]) + around(ext[now, p]) + base[p]
                new = total * inv[p]
                if k == SWEEPS - 1:
                    plain[p - WIDTH] = new[:cy, :cz]
                else:
                    ext[later, p] = new

    def edge_sems(it, side):
        return (xsend_sem.at[it, side], xrecv_sem.at[it, side])

    def source_start(it, source):
        srcb[it, 0] = source[:8]
        srcb[it, 1] = source[8:]

        def send(side, parts):
            for src, place_at, count, dm, dn in parts:
                remote(
                    srcb.at[it, pl.ds(src, count)], src_in.at[it, pl.ds(place_at, count)],
                    edge_sems(it, side), beside(0, dm, dn),
                ).start()

        send(0, ((0, 0, 1, -1, 0), (1, 1, 1, 1, 0)))

        @pl.when(n > 0)
        def _():
            send(1, ((0, 2, 2, 0, -1), (0, 4, 1, -1, -1), (1, 5, 1, 1, -1)))

        @pl.when(n < n_n - 1)
        def _():
            send(2, ((0, 6, 2, 0, 1), (0, 8, 1, -1, 1), (1, 9, 1, 1, 1)))

    def source_done(it):
        wait_recv(src_in.at[it, pl.ds(0, 2)], edge_sems(it, 0))

        @pl.when(n < n_n - 1)
        def _():
            wait_recv(src_in.at[it, pl.ds(2, 4)], edge_sems(it, 1))

        @pl.when(n > 0)
        def _():
            wait_recv(src_in.at[it, pl.ds(6, 4)], edge_sems(it, 2))

        def corner(up, down):
            return jnp.where(row8 < WIDTH, src_in[it, up], src_in[it, down])

        def lanes(after, before):
            return jnp.where(lane8 < WIDTH, after, before)

        main = jnp.concatenate([srcb[it, 0], srcb[it, 1], corner(0, 1)], axis=0)
        sides = jnp.concatenate(
            [lanes(src_in[it, 2], src_in[it, 6]), lanes(src_in[it, 3], src_in[it, 7]), lanes(corner(4, 5), corner(8, 9))],
            axis=0,
        )
        return jnp.concatenate([main, sides], axis=1)

    def grown(wide_source, have, p):
        total = jnp.zeros((24, 2 * cz), F32)
        if p == 0:
            total = wide_source
        for q in (p - 1, p + 1):
            if q in have:
                total = total + have[q]
        if p in have:
            total = total + around(have[p])
        return total * inv[WIDTH + p]

    def first_sweeps(wide_source):
        one = {0: wide_source * inv[WIDTH]}
        two = {p: grown(wide_source, one, p) for p in (0, -1, 1)}
        three = {p: grown(wide_source, two, p) for p in (0, -1, 1)}
        wall = grown(wide_source, three, 0)[:cy, :cz]
        return two, three, wall

    def last_sweeps(it, wide_source, two, three):
        three.update({p: grown(wide_source, two, p) for p in (-2, 2)})
        for p in (-3, -2, -1):
            lower[it, p + 3] = grown(wide_source, three, p)[:cy, :cz]
        remote(lower.at[it], lower_in.at[it], (lsend_sem.at[it], lrecv_sem.at[it]), beside(-1, 0, 0)).start()
        return [grown(wide_source, three, p)[:cy, :cz] for p in (1, 2, 3)]

    def lower_arrived(it):
        wait_recv(lower_in.at[it], (lsend_sem.at[it], lrecv_sem.at[it]))

    def apply(v16):
        v = v16.astype(F32)
        linked = jnp.dot(v16, col_hot[...], preferred_element_type=F32)
        near0, near1 = linked[:, :128], linked[:, 128:]

        def rows(t, carry):
            sums = []
            for u in range(8):
                i = t * 8 + u
                prod = selfb[i].astype(F32) * v + linkb[0, i].astype(F32) * near0 + linkb[1, i].astype(F32) * near1
                sums.append(jnp.sum(prod, axis=0, keepdims=True))
            kv[pl.ds(pl.multiple_of(t * 8, 8), 8), :] = jnp.concatenate(sums, axis=0)
            return carry

        lax.fori_loop(0, BLOCK // 8, rows, 0)
        return kv[...]

    def newton_start():
        mt, st = melt[...], state[...]
        bulk = BULK_BASE * jnp.exp(-BULK_SLOPE * mt)
        growth = jnp.exp(st)
        press = bulk * (growth - 1.0)
        base_volume = jnp.exp(EXPAND * mt)
        volume = base_volume * (1.0 - TAIT_C * st)
        sl = bulk * growth
        slope[...] = sl
        jd = diag[...] * sl + TAIT_C * base_volume
        jdiag[...] = jd
        res = apply(press.astype(BF16)) + (target[...] - volume) - inflow[...]
        resid[...] = res
        upd[...] = -res / jd

    def newton_step():
        weighted = (slope[...] * upd[...]).astype(BF16)
        linked = apply(weighted) - diag[...] * weighted.astype(F32)
        upd[...] = (-resid[...] - linked) / jdiag[...]

    for load in loads[:4]:
        load.wait()
    rel = jnp.bitwise_xor(owner[...], w)
    place = rel * 16 + slot[...] // 2
    half = slot[...] % 2
    faces = lax.broadcasted_iota(jnp.int32, (512, 128), 0)
    hot32 = jnp.where(faces == place, 1.0, 0.0)
    hot[...] = hot32.astype(BF16)
    terms = scatter_terms((coef[...] * melt[...], coef[...]))
    for it in range(ITERS):
        src_in[it] = jnp.zeros((10, 8, cz), F32)
    loads[4].wait()
    tab[0, 0, 0] = near[0, WIDTH]
    pl.semaphore_wait(barrier, len(peers))

    scatter_start(0, terms)
    loads[5].wait()
    send_low(0)
    send_high(0)
    gather_start(0)
    send_edges(0, 0)
    gather_on(0, 0)
    hot_t[...] = hot32.T.astype(BF16)
    scatter_on(0, 2)
    scatter_on(0, 1)
    scatter_on(0, 3)
    for load in loads[6:]:
        load.wait()
    froms = lax.broadcasted_iota(jnp.int32, (128, 128), 0)
    for k in range(2):
        col_hot[:, k * 128:(k + 1) * 128] = jnp.where(froms == columns[k:k + 1, :], 1.0, 0.0).astype(BF16)
    z_arrived(0, 1)
    z_arrived(0, 3)
    wide_arrived(0)
    z_arrived(0, 2)
    scatter_on(0, 0)
    square = coef[...] * coef[...]
    scatter_start(1, scatter_terms((square * melt[...], square)))
    take_edges(0, 0, (ext.at[0], inv))

    sum_a, sum_b = scatter_done(0)
    first_wall = near[0, WIDTH]
    source_start(0, sum_a - sum_b * first_wall)
    take_edges(0, 1, (ext.at[0], inv))
    prepare()
    plain_sweeps()
    spread_source = source_done(0)
    two, three, wall_part = first_sweeps(spread_source)
    second_wall = plain[0] + wall_part
    tab[1, 0, 0] = second_wall
    gather_start(1)
    upper = last_sweeps(0, spread_source, two, three)
    near[2, WIDTH] = second_wall
    for p in range(1, 4):
        near[2, WIDTH + p] = plain[p] + upper[p - 1]
    send_low(1)
    gather_on(1, 0)
    for p in range(4, cx - 3):
        near[2, WIDTH + p] = plain[p]
    for k in FAR_FIRST + (0,):
        scatter_on(1, k)

    def pick(t, carry):
        sums = []
        for u in range(8):
            i = t * 8 + u
            mask = lax.broadcasted_iota(jnp.int32, (BLOCK, 128), 0) == i
            sums.append(jnp.sum(jnp.where(mask, selfb[i].astype(F32), 0.0), axis=0, keepdims=True))
        diag[pl.ds(pl.multiple_of(t * 8, 8), 8), :] = jnp.concatenate(sums, axis=0)
        return carry

    lax.fori_loop(0, BLOCK // 8, pick, 0)
    cool(0)
    newton_start()
    z_arrived(1, 1)
    z_arrived(1, 3)
    lower_arrived(0)
    for p in range(3):
        near[2, WIDTH + cx - 3 + p] = plain[cx - 3 + p] + lower_in[0, p]
    send_high(1)
    send_edges(1, 0)
    newton_step()
    z_arrived(1, 2)
    newton_step()
    state[...] = state[...] + upd[...]

    sum_c, sum_d = scatter_done(1)
    source_start(1, sum_a - COOLING * sum_c + COOLING * sum_d * first_wall - sum_b * second_wall)
    wide_arrived(1)
    take_edges(1, 0, (ext.at[0],))
    cool(1)
    newton_start()
    spread_source = source_done(1)
    two, three, wall_part = first_sweeps(spread_source)
    upper = last_sweeps(1, spread_source, two, three)
    newton_step()
    take_edges(1, 1, (ext.at[0],))
    for p in range(planes):
        ext[0, p] = jnp.where(inv[p] > 0.0, ext[0, p], 0.0)
    plain_sweeps()
    out_field[0] = plain[0] + wall_part
    for p in range(1, 4):
        out_field[p] = plain[p] + upper[p - 1]
    for p in range(4, cx - 3):
        out_field[p] = plain[p]
    newton_step()
    mt, st = melt[...], state[...] + upd[...]
    out_press[...] = BULK_BASE * jnp.exp(-BULK_SLOPE * mt) * (jnp.exp(st) - 1.0)
    out_shrink[...] = 1.0 - jnp.exp(EXPAND * mt) * (1.0 - TAIT_C * st)
    lower_arrived(1)
    for p in range(3):
        out_field[cx - 3 + p] = plain[cx - 3 + p] + lower_in[1, p]

    def wait_send(region, sems):
        remote(region, region, sems, beside(0, 1, 0)).wait_send()

    for it in range(ITERS):
        for k in range(4):
            if k > 0:
                wait_send(tab.at[it, k, 0], z_sems(it, k))
                wait_send(psum.at[it, k], sum_sems(it, k))
            wait_send(tab.at[it, k, pl.ds(1, 7)], gather_sems(it, k))
            wait_send(spread.at[it, k, pl.ds(1, 7)], scatter_sems(it, k))
        wait_send(src_in.at[it, pl.ds(0, 2)], edge_sems(it, 0))

        @pl.when(n > 0)
        def _():
            wait_send(src_in.at[it, pl.ds(2, 4)], edge_sems(it, 1))

        @pl.when(n < n_n - 1)
        def _():
            wait_send(src_in.at[it, pl.ds(6, 4)], edge_sems(it, 2))

        wait_send(lower.at[it], (lsend_sem.at[it], lrecv_sem.at[it]))
    for g in range(2):
        some = group(g)
        wait_send(near.at[some, pl.ds(0, WIDTH)], h_sems(g, 0, 0))
        wait_send(near.at[some, pl.ds(0, WIDTH)], h_sems(g, 0, 1))
        for step, regions in ((0, (rows_own, lanes_own, corner_own)), (1, (rows_ghost, lanes_ghost, corner_ghost))):
            for kind, region in enumerate(regions):
                wait_send(region.at[some], h_sems(g, step, 2 + kind))


def per_device(
    mold_temp, capacity, melt_temp, log_pressure, target_volume, inflow, self_blocks, link_blocks,
    link_columns, wall_owner, wall_slot, transfer_coef,
):
    cx, cy, cz = mold_temp.shape
    cells, blocks = melt_temp.shape
    planes = cx + 2 * WIDTH
    vmem = pl.BlockSpec(memory_space=pltpu.VMEM)
    hbm = pl.BlockSpec(memory_space=pltpu.HBM)

    def scratch(*shape):
        return pltpu.VMEM(shape, F32)

    cav = scratch(cells, blocks)
    return pl.pallas_call(
        kernel,
        out_shape=(
            pltpu.VMEM(mold_temp.shape, F32),
            pltpu.VMEM(melt_temp.shape, F32),
            pltpu.VMEM(melt_temp.shape, F32),
        ),
        in_specs=[hbm] * 12,
        out_specs=(vmem, vmem, vmem),
        scratch_shapes=[
            pltpu.VMEM(self_blocks.shape, BF16),
            pltpu.VMEM(link_blocks.shape, BF16),
            scratch(ITERS, 4, 8, 16, 128),
            scratch(2, 4, 8, 2, 16, 128),
            scratch(2, 4, 8, 2, 16, 128),
            scratch(2, 4, 2, 16, 128),
            scratch(2, 4, 2, 16, 128),
            scratch(3, planes, cy, cz),
            scratch(3, 2, 8, 8, cz),
            scratch(3, 2, 4, 8, cz),
            scratch(3, 2, 8, cz),
            scratch(3, 2, 8, cz),
            scratch(3, 2, 8, 8, cz),
            scratch(3, 2, 4, 8, cz),
            scratch(3, 2, 2, 8, cz),
            scratch(3, 2, 2, 8, cz),
            scratch(3, 2, 2, 8, cz),
            scratch(3, 2, 2, 8, cz),
            scratch(2, planes, 24, 2 * cz),
            scratch(planes, 24, 2 * cz),
            scratch(planes, 24, 2 * cz),
            scratch(cx, cy, cz),
            scratch(ITERS, 2, 8, cz),
            scratch(ITERS, 10, 8, cz),
            scratch(ITERS, 3, cy, cz),
            scratch(ITERS, 3, cy, cz),
            pltpu.VMEM((512, 128), BF16),
            pltpu.VMEM((128, 512), BF16),
            pltpu.VMEM((128, 256), BF16),
            cav, cav, cav, cav, cav, cav, cav, cav, cav, cav, cav,
            pltpu.VMEM((2, blocks), jnp.int32),
            pltpu.VMEM((1, blocks), jnp.int32),
            pltpu.VMEM((1, blocks), jnp.int32),
            pltpu.SemaphoreType.DMA((12,)),
            *[pltpu.SemaphoreType.DMA((ITERS, 4))] * 8,
            *[pltpu.SemaphoreType.DMA((ITERS, 3))] * 2,
            *[pltpu.SemaphoreType.DMA((ITERS,))] * 2,
            *[pltpu.SemaphoreType.DMA((2, 2, 5))] * 2,
        ],
        compiler_params=pltpu.CompilerParams(
            collective_id=0, has_side_effects=True, vmem_limit_bytes=56 * 1024 * 1024
        ),
    )(
        mold_temp, capacity, melt_temp, log_pressure, target_volume, inflow, transfer_coef,
        link_columns, wall_owner.reshape(1, blocks), wall_slot.reshape(1, blocks), self_blocks, link_blocks,
    )


def solution(mesh):
    cavity = P(None, ("wide", "mid", "narrow"))
    brick = P("wide", "mid", "narrow")
    flat = P(("wide", "mid", "narrow"))
    return jax.shard_map(
        per_device,
        mesh=mesh,
        in_specs=(
            brick, brick, cavity, cavity, cavity, cavity,
            P(None, None, ("wide", "mid", "narrow")),
            P(None, None, None, ("wide", "mid", "narrow")),
            cavity, flat, flat, cavity,
        ),
        out_specs=(brick, cavity, cavity),
        check_vma=False,
    )
```

time: 596 us -> 58 us (0.10); the launches traced: 588 us -> 57.9 us
  waiting for transfers between devices: 211 us -> 0 us
  starting transfers between devices: 174 us -> 0 us
  blocking collectives: 102 us -> 0 us
  Pallas kernels: 0 us -> 55.3 us
  other arithmetic: 45.8 us -> 0 us
  local copies, waits for them, and re-layouts: 39.7 us -> 1.89 us
  between operations: 15.4 us -> 0.64 us
    reduce_scatter x2 -> x0, waiting for transfers between devices: 183 us -> none  [per_device(): lax.psum_scatter(spread, 'wide', scatter_dimension=1, tiled=True)]
    ppermute x48 -> x0, starting transfers between devices: 174 us -> none  [the longest x24 133 us: padded_2(): before = lax.ppermute(last, axis, up)]
    all_gather x2 -> x0, blocking collectives: 102 us -> none  [per_device(): table = lax.all_gather(columns, 'wide', axis=1, tiled=True)]
    pallas_call x0 -> x1, Pallas kernels: none -> 55.3 us  [per_device(): pl.pallas_call(kernel, out_shape=(pltpu.VMEM(mold_temp.shape, F32), pltpu...]
    ppermute x48 -> x0, waiting for transfers between devices: 27.7 us -> none  [the longest x24 24 us: padded_2(): after = lax.ppermute(leading, axis, down)]
    dot_general x12 -> x0, other arithmetic: 14.2 us -> none  [the longest x6 10.1 us: block_apply(): jnp.einsum('nijb,jnb->ib', link_blocks, nearby, preferred_element_type=jn...]
    gather x11 -> x0, local copies, waits for them, and re-layouts: 14.1 us -> none  [the longest x6 10.1 us: block_apply(): nearby = values[:, link_columns]]
    unnamed x132 -> x3, local copies, waits for them, and re-layouts: 12.8 us -> 1.89 us
  transfers between devices with their start and end apart: 50 -> 0, of which waited for: 15 -> 0; matrix products, arithmetic and copies ran while one was open for 10% -> 0% of each run, Pallas kernels for 0% -> 0%
where the time goes in v2:
time: 58 us; the launch traced here: 57.9 us
  Pallas kernels  55.3 us (95%)
  local copies, waits for them, and re-layouts  1.89 us (3%)
  between operations  0.64 us (1%)
    pallas_call x1, Pallas kernels, per_device(): pl.pallas_call(kernel, out_shape=(pltpu.VMEM(mold_temp.shape, F32), pltpu...  55.3 us
    unnamed x3, local copies, waits for them, and re-layouts  1.89 us

profile of v2, /device:TPU:7, one launch (start us, length us, event | category | flops | bytes accessed | tf_op | source)
XLA Modules:
  0.0 57.9 jit_solution(1383899404258821591)
XLA Ops:
  0.6 55.3 %shard_map.139 = (f32[16,16,128]{2,1,0:T(8,128)S(1)}, f32[64,128]{1,0:T(8,128)S(1)}, f32[64,128]{1,0:T(8,128)S(1)}) custom-call(f32[16,16,128]{2,1,0:T(8,128)} %mold.1, f32[16,16,128]{2,1,0:T(8,128)} %cap.1, f32[64,128]{1,0:T(8,128)} %melt_in.1, f32[64,128]{1,0:T(8,128)} %logp.1, f32[64,128]{1,0:T(8,128)} %target_in.1, f32[64,128]{1,0:T(8,128)} %inflow_in.1, ...), custom_call_target="tpu_custom_call" | custom-call | tf_op jit(solution)/shard_map/pallas_call | solution.py:556
  56.0 0.7 %copy.18 = f32[16,16,128]{2,1,0:T(8,128)} copy(f32[16,16,128]{2,1,0:T(8,128)S(1)} %get-tuple-element.3) | data formatting | bytes 262144
  56.6 0.6 %copy.19 = f32[64,128]{1,0:T(8,128)} copy(f32[64,128]{1,0:T(8,128)S(1)} %get-tuple-element.4) | data formatting | bytes 65536
  57.2 0.6 %copy.20 = f32[64,128]{1,0:T(8,128)} copy(f32[64,128]{1,0:T(8,128)S(1)} %get-tuple-element.5) | data formatting | bytes 65536

commit v3 on v2

--- a/solution.py
+++ b/solution.py
@@ -140,16 +140,18 @@
             parts.extend(split_terms(placed))
         return jnp.concatenate(parts, axis=0)
 
-    def scatter_start(a, terms):
-        for k in FAR_FIRST + (0,):
+    def scatter_fill(a, terms):
+        for k in range(4):
             summed = lax.dot_general(
                 hot[k * 128:(k + 1) * 128, :], terms, (((1,), (1,)), ((), ())), preferred_element_type=F32
             )
             for q in range(2):
                 one = summed[:, 256 * q:256 * q + 128] + summed[:, 256 * q + 128:256 * q + 256]
                 spread[a, k, :, q] = one.reshape(8, 16, 128)
-            for j in range(1, 8):
-                remote(spread.at[a, k, j], rs1.at[a, k, j], scatter_sems(a, k), xc_peer(j)).start()
+
+    def scatter_start(a, k):
+        for j in range(1, 8):
+            remote(spread.at[a, k, j], rs1.at[a, k, j], scatter_sems(a, k), xc_peer(j)).start()
 
     def scatter_on(a, k):
         wait_recv(rs1.at[a, k, pl.ds(1, 7)], scatter_sems(a, k))
@@ -191,11 +193,8 @@
             near.at[group(g), pl.ds(cx, WIDTH)], near.at[group(g), pl.ds(0, WIDTH)], h_sems(g, 0, 1), beside(1, 0, 0)
         ).start()
 
-    def send_edges(g, step):
-        which, row_out, lane_out, rows_in, lanes_in, corner_in = (
-            (own_planes, row_own, lane_own, rows_own, lanes_own, corner_own),
-            (ghost_planes, row_ghost, lane_ghost, rows_ghost, lanes_ghost, corner_ghost),
-        )[step]
+    def pack_edges(g, step):
+        which, row_out, lane_out = ((own_planes, row_own, lane_own), (ghost_planes, row_ghost, lane_ghost))[step]
         for a in arrays[g]:
             packed = jnp.zeros((cy, cz), F32)
             for q, p in enumerate(which):
@@ -207,6 +206,12 @@
                 one, two = near[a, which[q]], near[a, which[q + 2]]
                 row_out[a, 0, t] = jnp.where(row8 < WIDTH, one[:8], pltpu.roll(two[:8], 4, 0))
                 row_out[a, 1, t] = jnp.where(row8 < WIDTH, pltpu.roll(one[8:], 4, 0), two[8:])
+
+    def send_edges(g, step):
+        row_out, lane_out, rows_in, lanes_in, corner_in = (
+            (row_own, lane_own, rows_own, lanes_own, corner_own),
+            (row_ghost, lane_ghost, rows_ghost, lanes_ghost, corner_ghost),
+        )[step]
         some = group(g)
         for side, dm in ((0, -1), (1, 1)):
             remote(row_out.at[some, side], rows_in.at[some, side], h_sems(g, step, 2), beside(0, dm, 0)).start()
@@ -246,6 +251,7 @@
     def wide_arrived(g):
         wait_recv(near.at[group(g), pl.ds(WIDTH + cx, WIDTH)], h_sems(g, 0, 0))
         wait_recv(near.at[group(g), pl.ds(0, WIDTH)], h_sems(g, 0, 1))
+        pack_edges(g, 1)
         send_edges(g, 1)
 
     def prepare():
@@ -387,14 +393,14 @@
         slope[...] = sl
         jd = diag[...] * sl + TAIT_C * base_volume
         jdiag[...] = jd
-        res = apply(press.astype(BF16)) + (target[...] - volume) - inflow[...]
+        rounded = press.astype(BF16)
+        res = apply(rounded) + diag[...] * rounded.astype(F32) + (target[...] - volume) - inflow[...]
         resid[...] = res
         upd[...] = -res / jd
 
     def newton_step():
         weighted = (slope[...] * upd[...]).astype(BF16)
-        linked = apply(weighted) - diag[...] * weighted.astype(F32)
-        upd[...] = (-resid[...] - linked) / jdiag[...]
+        upd[...] = (-resid[...] - apply(weighted)) / jdiag[...]
 
     for load in loads[:4]:
         load.wait()
@@ -404,41 +410,58 @@
     faces = lax.broadcasted_iota(jnp.int32, (512, 128), 0)
     hot32 = jnp.where(faces == place, 1.0, 0.0)
     hot[...] = hot32.astype(BF16)
-    terms = scatter_terms((coef[...] * melt[...], coef[...]))
+    scatter_fill(0, scatter_terms((coef[...] * melt[...], coef[...])))
     for it in range(ITERS):
         src_in[it] = jnp.zeros((10, 8, cz), F32)
     loads[4].wait()
+    loads[5].wait()
     tab[0, 0, 0] = near[0, WIDTH]
+    pack_edges(0, 0)
     pl.semaphore_wait(barrier, len(peers))
 
-    scatter_start(0, terms)
-    loads[5].wait()
+    for k in FAR_FIRST:
+        scatter_start(0, k)
     send_low(0)
     send_high(0)
     gather_start(0)
     send_edges(0, 0)
+    scatter_start(0, 0)
     gather_on(0, 0)
     hot_t[...] = hot32.T.astype(BF16)
-    scatter_on(0, 2)
-    scatter_on(0, 1)
-    scatter_on(0, 3)
     for load in loads[6:]:
         load.wait()
     froms = lax.broadcasted_iota(jnp.int32, (128, 128), 0)
     for k in range(2):
         col_hot[:, k * 128:(k + 1) * 128] = jnp.where(froms == columns[k:k + 1, :], 1.0, 0.0).astype(BF16)
+
+    def pick(t, carry):
+        sums = []
+        for u in range(8):
+            i = t * 8 + u
+            mask = lax.broadcasted_iota(jnp.int32, (BLOCK, 128), 0) == i
+            block = selfb[i].astype(F32)
+            sums.append(jnp.sum(jnp.where(mask, block, 0.0), axis=0, keepdims=True))
+            selfb[i] = jnp.where(mask, 0.0, block).astype(BF16)
+        diag[pl.ds(pl.multiple_of(t * 8, 8), 8), :] = jnp.concatenate(sums, axis=0)
+        return carry
+
+    lax.fori_loop(0, BLOCK // 8, pick, 0)
+    for k in FAR_FIRST:
+        scatter_on(0, k)
+    square = coef[...] * coef[...]
+    scatter_fill(1, scatter_terms((square * melt[...], square)))
     z_arrived(0, 1)
     z_arrived(0, 3)
     wide_arrived(0)
-    z_arrived(0, 2)
+    for k in FAR_FIRST + (0,):
+        scatter_start(1, k)
+    take_edges(0, 0, (ext.at[0], inv))
     scatter_on(0, 0)
-    square = coef[...] * coef[...]
-    scatter_start(1, scatter_terms((square * melt[...], square)))
-    take_edges(0, 0, (ext.at[0], inv))
 
     sum_a, sum_b = scatter_done(0)
     first_wall = near[0, WIDTH]
     source_start(0, sum_a - sum_b * first_wall)
+    z_arrived(0, 2)
     take_edges(0, 1, (ext.at[0], inv))
     prepare()
     plain_sweeps()
@@ -447,27 +470,17 @@
     second_wall = plain[0] + wall_part
     tab[1, 0, 0] = second_wall
     gather_start(1)
+    gather_on(1, 0)
     upper = last_sweeps(0, spread_source, two, three)
     near[2, WIDTH] = second_wall
     for p in range(1, 4):
         near[2, WIDTH + p] = plain[p] + upper[p - 1]
     send_low(1)
-    gather_on(1, 0)
+    for k in FAR_FIRST + (0,):
+        scatter_on(1, k)
     for p in range(4, cx - 3):
         near[2, WIDTH + p] = plain[p]
-    for k in FAR_FIRST + (0,):
-        scatter_on(1, k)
-
-    def pick(t, carry):
-        sums = []
-        for u in range(8):
-            i = t * 8 + u
-            mask = lax.broadcasted_iota(jnp.int32, (BLOCK, 128), 0) == i
-            sums.append(jnp.sum(jnp.where(mask, selfb[i].astype(F32), 0.0), axis=0, keepdims=True))
-        diag[pl.ds(pl.multiple_of(t * 8, 8), 8), :] = jnp.concatenate(sums, axis=0)
-        return carry
-
-    lax.fori_loop(0, BLOCK // 8, pick, 0)
+
     cool(0)
     newton_start()
     z_arrived(1, 1)
@@ -476,22 +489,22 @@
     for p in range(3):
         near[2, WIDTH + cx - 3 + p] = plain[cx - 3 + p] + lower_in[0, p]
     send_high(1)
+    pack_edges(1, 0)
     send_edges(1, 0)
     newton_step()
+    sum_c, sum_d = scatter_done(1)
+    source_start(1, sum_a - COOLING * sum_c + COOLING * sum_d * first_wall - sum_b * second_wall)
     z_arrived(1, 2)
     newton_step()
     state[...] = state[...] + upd[...]
-
-    sum_c, sum_d = scatter_done(1)
-    source_start(1, sum_a - COOLING * sum_c + COOLING * sum_d * first_wall - sum_b * second_wall)
     wide_arrived(1)
     take_edges(1, 0, (ext.at[0],))
-    cool(1)
-    newton_start()
     spread_source = source_done(1)
     two, three, wall_part = first_sweeps(spread_source)
     upper = last_sweeps(1, spread_source, two, three)
-    newton_step()
+
+    cool(1)
+    newton_start()
     take_edges(1, 1, (ext.at[0],))
     for p in range(planes):
         ext[0, p] = jnp.where(inv[p] > 0.0, ext[0, p], 0.0)
@@ -502,12 +515,13 @@
     for p in range(4, cx - 3):
         out_field[p] = plain[p]
     newton_step()
+    lower_arrived(1)
+    for p in range(3):
+        out_field[cx - 3 + p] = plain[cx - 3 + p] + lower_in[1, p]
+    newton_step()
     mt, st = melt[...], state[...] + upd[...]
     out_press[...] = BULK_BASE * jnp.exp(-BULK_SLOPE * mt) * (jnp.exp(st) - 1.0)
     out_shrink[...] = 1.0 - jnp.exp(EXPAND * mt) * (1.0 - TAIT_C * st)
-    lower_arrived(1)
-    for p in range(3):
-        out_field[cx - 3 + p] = plain[cx - 3 + p] + lower_in[1, p]
 
     def wait_send(region, sems):
         remote(region, region, sems, beside(0, 1, 0)).wait_send()

time: 58 us -> 58.1 us (level)
  no operation moved by 1% of the time
where the time goes in v3:
time: 58.1 us; the launch traced here: 58 us
  Pallas kernels  55.5 us (96%)
  local copies, waits for them, and re-layouts  1.89 us (3%)
  between operations  0.64 us (1%)
    pallas_call x1, Pallas kernels, per_device(): pl.pallas_call(kernel, out_shape=(pltpu.VMEM(mold_temp.shape, F32), pltpu...  55.5 us
    unnamed x3, local copies, waits for them, and re-layouts  1.89 us

profile of v3, /device:TPU:7, one launch (start us, length us, event | category | flops | bytes accessed | tf_op | source)
XLA Modules:
  0.0 58.0 jit_solution(975072070839753910)
XLA Ops:
  0.6 55.5 %shard_map.139 = (f32[16,16,128]{2,1,0:T(8,128)S(1)}, f32[64,128]{1,0:T(8,128)S(1)}, f32[64,128]{1,0:T(8,128)S(1)}) custom-call(f32[16,16,128]{2,1,0:T(8,128)} %mold.1, f32[16,16,128]{2,1,0:T(8,128)} %cap.1, f32[64,128]{1,0:T(8,128)} %melt_in.1, f32[64,128]{1,0:T(8,128)} %logp.1, f32[64,128]{1,0:T(8,128)} %target_in.1, f32[64,128]{1,0:T(8,128)} %inflow_in.1, ...), custom_call_target="tpu_custom_call" | custom-call | tf_op jit(solution)/shard_map/pallas_call | solution.py:570
  56.1 0.7 %copy.18 = f32[16,16,128]{2,1,0:T(8,128)} copy(f32[16,16,128]{2,1,0:T(8,128)S(1)} %get-tuple-element.3) | data formatting | bytes 262144
  56.8 0.6 %copy.19 = f32[64,128]{1,0:T(8,128)} copy(f32[64,128]{1,0:T(8,128)S(1)} %get-tuple-element.4) | data formatting | bytes 65536
  57.4 0.6 %copy.20 = f32[64,128]{1,0:T(8,128)} copy(f32[64,128]{1,0:T(8,128)S(1)} %get-tuple-element.5) | data formatting | bytes 65536

commit v4 on v3

--- a/solution.py
+++ b/solution.py
@@ -12,7 +12,7 @@
 SWEEPS = 4
 INNER = 2
 WIDTH = 4
-FAR_FIRST = (2, 1, 3)
+DISTANCE = (0, 1, 3, 2)
 
 CONDUCT = 1.0
 COOLING = 0.5
@@ -100,35 +100,36 @@
     def z_sems(it, k):
         return (zsend_sem.at[it, k], zrecv_sem.at[it, k])
 
-    def gather_sems(it, k):
-        return (gsend_sem.at[it, k], grecv_sem.at[it, k])
-
-    def gather_on(it, k):
+    def gather_sems(it, part):
+        return (gsend_sem.at[it, part], grecv_sem.at[it, part])
+
+    gather_parts = ((0, 3), (3, 1))
+    scatter_parts = ((3, 1), (1, 2), (0, 1))
+
+    def gather_start(it):
+        for k in (3, 1, 2):
+            remote(tab.at[it, 0, 0], tab.at[it, 0, k], z_sems(it, k), z_peer(DISTANCE[k])).start()
+
+    def gather_on(it, part):
+        first, count = gather_parts[part]
+        for k in range(max(first, 1), first + count):
+            wait_recv(tab.at[it, 0, k], z_sems(it, k))
         for j in range(1, 8):
-            remote(tab.at[it, k, 0], tab.at[it, k, j], gather_sems(it, k), xc_peer(j)).start()
-
-    def gather_start(it):
-        for k in FAR_FIRST:
-            remote(tab.at[it, 0, 0], tab.at[it, k, 0], z_sems(it, k), z_peer(k)).start()
-
-    def z_arrived(it, k):
-        wait_recv(tab.at[it, k, 0], z_sems(it, k))
-        gather_on(it, k)
+            remote(
+                tab.at[it, 0, pl.ds(first, count)], tab.at[it, j, pl.ds(first, count)], gather_sems(it, part), xc_peer(j)
+            ).start()
 
     def cool(it):
-        found = jnp.zeros((128, 256), F32)
-        for k in (0, 1, 3, 2):
-            wait_recv(tab.at[it, k, pl.ds(1, 7)], gather_sems(it, k))
-            hi, lo = split_terms(tab[it, k].reshape(128, 128))
-            found = found + jnp.dot(
-                hot_t[:, k * 128:(k + 1) * 128], jnp.concatenate([hi, lo], axis=1), preferred_element_type=F32
-            )
+        for part, (first, count) in enumerate(gather_parts):
+            wait_recv(tab.at[it, pl.ds(1, 7), pl.ds(first, count)], gather_sems(it, part))
+        hi, lo = split_terms(tab[it].reshape(512, 128))
+        found = jnp.dot(hot_t[...], jnp.concatenate([hi, lo], axis=1), preferred_element_type=F32)
         found = (found[:, :128] + found[:, 128:]).T
         wall = jnp.where(half == 1, found[BLOCK:], found[:BLOCK])
         melt[...] = melt[...] - COOLING * (coef[...] * (melt[...] - wall))
 
-    def scatter_sems(a, k):
-        return (csend_sem.at[a, k], crecv_sem.at[a, k])
+    def scatter_sems(a, part):
+        return (csend_sem.at[a, part], crecv_sem.at[a, part])
 
     def sum_sems(a, k):
         return (ysend_sem.at[a, k], yrecv_sem.at[a, k])
@@ -141,32 +142,37 @@
         return jnp.concatenate(parts, axis=0)
 
     def scatter_fill(a, terms):
-        for k in range(4):
+        for j in range(0, 8, 2):
             summed = lax.dot_general(
-                hot[k * 128:(k + 1) * 128, :], terms, (((1,), (1,)), ((), ())), preferred_element_type=F32
+                hot[j * 64:(j + 2) * 64, :], terms, (((1,), (1,)), ((), ())), preferred_element_type=F32
             )
             for q in range(2):
                 one = summed[:, 256 * q:256 * q + 128] + summed[:, 256 * q + 128:256 * q + 256]
-                spread[a, k, :, q] = one.reshape(8, 16, 128)
-
-    def scatter_start(a, k):
+                spread[a, j:j + 2, :, q] = one.reshape(2, 4, 16, 128)
+
+    def scatter_start(a, part):
+        first, count = scatter_parts[part]
         for j in range(1, 8):
-            remote(spread.at[a, k, j], rs1.at[a, k, j], scatter_sems(a, k), xc_peer(j)).start()
-
-    def scatter_on(a, k):
-        wait_recv(rs1.at[a, k, pl.ds(1, 7)], scatter_sems(a, k))
-        for q in range(2):
-            total = spread[a, k, 0, q]
-            for j in range(1, 8):
-                total = total + rs1[a, k, j, q]
-            psum[a, k, q] = total
-        if k > 0:
-            remote(psum.at[a, k], rs2.at[a, k], sum_sems(a, k), z_peer(k)).start()
+            remote(
+                spread.at[a, j, pl.ds(first, count)], rs1.at[a, j, pl.ds(first, count)], scatter_sems(a, part), xc_peer(j)
+            ).start()
+
+    def scatter_on(a, part):
+        first, count = scatter_parts[part]
+        wait_recv(rs1.at[a, pl.ds(1, 7), pl.ds(first, count)], scatter_sems(a, part))
+        for k in range(first, first + count):
+            for q in range(2):
+                total = spread[a, 0, k, q]
+                for j in range(1, 8):
+                    total = total + rs1[a, j, k, q]
+                psum[a, k, q] = total
+            if k > 0:
+                remote(psum.at[a, k], rs2.at[a, k], sum_sems(a, k), z_peer(DISTANCE[k])).start()
 
     def scatter_done(a):
-        for k in (1, 3, 2):
+        for k in (1, 2, 3):
             wait_recv(rs2.at[a, k], sum_sems(a, k))
-        return [((psum[a, 0, q] + rs2[a, 1, q]) + (rs2[a, 3, q] + rs2[a, 2, q])) for q in range(2)]
+        return [((psum[a, 0, q] + rs2[a, 1, q]) + (rs2[a, 2, q] + rs2[a, 3, q])) for q in range(2)]
 
     lane = lax.broadcasted_iota(jnp.int32, (cy, cz), 1)
     lane24 = lax.broadcasted_iota(jnp.int32, (24, cz), 1)
@@ -405,7 +411,8 @@
     for load in loads[:4]:
         load.wait()
     rel = jnp.bitwise_xor(owner[...], w)
-    place = rel * 16 + slot[...] // 2
+    rel_z = rel // 8
+    place = ((rel % 8) * 4 + jnp.bitwise_xor(rel_z, rel_z // 2)) * 16 + slot[...] // 2
     half = slot[...] % 2
     faces = lax.broadcasted_iota(jnp.int32, (512, 128), 0)
     hot32 = jnp.where(faces == place, 1.0, 0.0)
@@ -419,14 +426,13 @@
     pack_edges(0, 0)
     pl.semaphore_wait(barrier, len(peers))
 
-    for k in FAR_FIRST:
-        scatter_start(0, k)
+    scatter_start(0, 0)
+    scatter_start(0, 1)
     send_low(0)
     send_high(0)
     gather_start(0)
     send_edges(0, 0)
-    scatter_start(0, 0)
-    gather_on(0, 0)
+    scatter_start(0, 2)
     hot_t[...] = hot32.T.astype(BF16)
     for load in loads[6:]:
         load.wait()
@@ -446,45 +452,42 @@
         return carry
 
     lax.fori_loop(0, BLOCK // 8, pick, 0)
-    for k in FAR_FIRST:
-        scatter_on(0, k)
+    scatter_on(0, 0)
+    scatter_on(0, 1)
     square = coef[...] * coef[...]
     scatter_fill(1, scatter_terms((square * melt[...], square)))
-    z_arrived(0, 1)
-    z_arrived(0, 3)
+    gather_on(0, 0)
     wide_arrived(0)
-    for k in FAR_FIRST + (0,):
-        scatter_start(1, k)
+    for part in range(3):
+        scatter_start(1, part)
     take_edges(0, 0, (ext.at[0], inv))
-    scatter_on(0, 0)
+    scatter_on(0, 2)
 
     sum_a, sum_b = scatter_done(0)
     first_wall = near[0, WIDTH]
     source_start(0, sum_a - sum_b * first_wall)
-    z_arrived(0, 2)
+    gather_on(0, 1)
     take_edges(0, 1, (ext.at[0], inv))
     prepare()
     plain_sweeps()
+    for part in range(3):
+        scatter_on(1, part)
     spread_source = source_done(0)
     two, three, wall_part = first_sweeps(spread_source)
     second_wall = plain[0] + wall_part
     tab[1, 0, 0] = second_wall
     gather_start(1)
-    gather_on(1, 0)
     upper = last_sweeps(0, spread_source, two, three)
     near[2, WIDTH] = second_wall
     for p in range(1, 4):
         near[2, WIDTH + p] = plain[p] + upper[p - 1]
     send_low(1)
-    for k in FAR_FIRST + (0,):
-        scatter_on(1, k)
     for p in range(4, cx - 3):
         near[2, WIDTH + p] = plain[p]
 
     cool(0)
     newton_start()
-    z_arrived(1, 1)
-    z_arrived(1, 3)
+    gather_on(1, 0)
     lower_arrived(0)
     for p in range(3):
         near[2, WIDTH + cx - 3 + p] = plain[cx - 3 + p] + lower_in[0, p]
@@ -494,7 +497,7 @@
     newton_step()
     sum_c, sum_d = scatter_done(1)
     source_start(1, sum_a - COOLING * sum_c + COOLING * sum_d * first_wall - sum_b * second_wall)
-    z_arrived(1, 2)
+    gather_on(1, 1)
     newton_step()
     state[...] = state[...] + upd[...]
     wide_arrived(1)
@@ -527,12 +530,13 @@
         remote(region, region, sems, beside(0, 1, 0)).wait_send()
 
     for it in range(ITERS):
-        for k in range(4):
-            if k > 0:
-                wait_send(tab.at[it, k, 0], z_sems(it, k))
-                wait_send(psum.at[it, k], sum_sems(it, k))
-            wait_send(tab.at[it, k, pl.ds(1, 7)], gather_sems(it, k))
-            wait_send(spread.at[it, k, pl.ds(1, 7)], scatter_sems(it, k))
+        for k in range(1, 4):
+            wait_send(tab.at[it, 0, k], z_sems(it, k))
+            wait_send(psum.at[it, k], sum_sems(it, k))
+        for part, (first, count) in enumerate(gather_parts):
+            wait_send(tab.at[it, pl.ds(1, 7), pl.ds(first, count)], gather_sems(it, part))
+        for part, (first, count) in enumerate(scatter_parts):
+            wait_send(spread.at[it, pl.ds(1, 7), pl.ds(first, count)], scatter_sems(it, part))
         wait_send(src_in.at[it, pl.ds(0, 2)], edge_sems(it, 0))
 
         @pl.when(n > 0)
@@ -579,9 +583,9 @@
         scratch_shapes=[
             pltpu.VMEM(self_blocks.shape, BF16),
             pltpu.VMEM(link_blocks.shape, BF16),
-            scratch(ITERS, 4, 8, 16, 128),
-            scratch(2, 4, 8, 2, 16, 128),
-            scratch(2, 4, 8, 2, 16, 128),
+            scratch(ITERS, 8, 4, 16, 128),
+            scratch(2, 8, 4, 2, 16, 128),
+            scratch(2, 8, 4, 2, 16, 128),
             scratch(2, 4, 2, 16, 128),
             scratch(2, 4, 2, 16, 128),
             scratch(3, planes, cy, cz),

time: 58.1 us -> 59.1 us (1.017)
  Pallas kernels: 55.5 us -> 56.5 us
    pallas_call x1, Pallas kernels: 55.5 us -> 56.5 us  [per_device(): pl.pallas_call(kernel, out_shape=(pltpu.VMEM(mold_temp.shape, F32), pltpu...]
where the time goes in v4:
time: 59.1 us; the launch traced here: 59 us
  Pallas kernels  56.5 us (96%)
  local copies, waits for them, and re-layouts  1.89 us (3%)
  between operations  0.64 us (1%)
    pallas_call x1, Pallas kernels, per_device(): pl.pallas_call(kernel, out_shape=(pltpu.VMEM(mold_temp.shape, F32), pltpu...  56.5 us
    unnamed x3, local copies, waits for them, and re-layouts  1.89 us

profile of v4, /device:TPU:7, one launch (start us, length us, event | category | flops | bytes accessed | tf_op | source)
XLA Modules:
  0.0 59.0 jit_solution(13380600183115128579)
XLA Ops:
  0.6 56.5 %shard_map.139 = (f32[16,16,128]{2,1,0:T(8,128)S(1)}, f32[64,128]{1,0:T(8,128)S(1)}, f32[64,128]{1,0:T(8,128)S(1)}) custom-call(f32[16,16,128]{2,1,0:T(8,128)} %mold.1, f32[16,16,128]{2,1,0:T(8,128)} %cap.1, f32[64,128]{1,0:T(8,128)} %melt_in.1, f32[64,128]{1,0:T(8,128)} %logp.1, f32[64,128]{1,0:T(8,128)} %target_in.1, f32[64,128]{1,0:T(8,128)} %inflow_in.1, ...), custom_call_target="tpu_custom_call" | custom-call | tf_op jit(solution)/shard_map/pallas_call | solution.py:574
  57.1 0.7 %copy.18 = f32[16,16,128]{2,1,0:T(8,128)} copy(f32[16,16,128]{2,1,0:T(8,128)S(1)} %get-tuple-element.3) | data formatting | bytes 262144
  57.8 0.6 %copy.19 = f32[64,128]{1,0:T(8,128)} copy(f32[64,128]{1,0:T(8,128)S(1)} %get-tuple-element.4) | data formatting | bytes 65536
  58.4 0.6 %copy.20 = f32[64,128]{1,0:T(8,128)} copy(f32[64,128]{1,0:T(8,128)S(1)} %get-tuple-element.5) | data formatting | bytes 65536

commit v5 on v3

--- a/solution.py
+++ b/solution.py
@@ -45,7 +45,7 @@
 def kernel(
     mold, cap, melt_in, logp, target_in, inflow_in, coef_in, columns_in, owner_in, slot_in, self_in, link_in,
     out_field, out_press, out_shrink,
-    selfb, linkb, tab, spread, rs1, psum, rs2, near,
+    selfb, linkb, wide_blocks, tab, spread, rs1, psum, rs2, near,
     row_own, row_ghost, lane_own, lane_ghost, rows_own, rows_ghost, lanes_own, lanes_ghost, corner_own, corner_ghost,
     ext, inv, base, plain, srcb, src_in, lower, lower_in,
     hot, hot_t, col_hot, diag, kv, resid, jdiag, slope, upd, state, melt, target, inflow, coef,
@@ -254,7 +254,7 @@
         pack_edges(g, 1)
         send_edges(g, 1)
 
-    def prepare():
+    def prepare(which):
         row_at = lax.broadcasted_iota(jnp.int32, (24, 2 * cz), 0)
         row_at = jnp.where(row_at < cy + WIDTH, row_at, row_at - 24) + m * cy
         lane_at = lax.broadcasted_iota(jnp.int32, (24, 2 * cz), 1)
@@ -262,7 +262,7 @@
         lane_at = jnp.where(lane_at < cz + WIDTH, lane_at, lane_at - 2 * cz) + n * cz
         inside = lane_real & (row_at >= 0) & (row_at < n_m * cy) & (lane_at >= 0) & (lane_at < n_n * cz)
         inside = jnp.where(inside, 1.0, 0.0)
-        for p in range(planes):
+        for p in which:
             here = inside
             if p < WIDTH:
                 here = jnp.where(w > 0, inside, 0.0)
@@ -273,15 +273,20 @@
             inv[p] = here / (capacity + 6.0 * CONDUCT)
             ext[0, p] = jnp.where(here > 0.0, start, 0.0)
 
+    def keep_inside(which):
+        for p in which:
+            ext[0, p] = jnp.where(inv[p] > 0.0, ext[0, p], 0.0)
+
     def around(plane):
         rows = pltpu.roll(plane, 1, 0) + pltpu.roll(plane, 23, 0)
         return rows + (pltpu.roll(plane, 1, 1) + pltpu.roll(plane, 2 * cz - 1, 1))
 
-    def plain_sweeps():
+    def plain_sweeps(inner):
         for k in range(SWEEPS):
             now, later = k % 2, (k + 1) % 2
             edge = k + 1
-            for p in range(edge, planes - edge):
+            inside = range(edge + WIDTH, planes - edge - WIDTH)
+            for p in inside if inner else [p for p in range(edge, planes - edge) if p not in inside]:
                 total = (ext[now, p - 1] + ext[now, p + 1]) + around(ext[now, p]) + base[p]
                 new = total * inv[p]
                 if k == SWEEPS - 1:
@@ -374,7 +379,7 @@
             sums = []
             for u in range(8):
                 i = t * 8 + u
-                prod = selfb[i].astype(F32) * v + linkb[0, i].astype(F32) * near0 + linkb[1, i].astype(F32) * near1
+                prod = wide_blocks[0, i] * v + wide_blocks[1, i] * near0 + wide_blocks[2, i] * near1
                 sums.append(jnp.sum(prod, axis=0, keepdims=True))
             kv[pl.ds(pl.multiple_of(t * 8, 8), 8), :] = jnp.concatenate(sums, axis=0)
             return carry
@@ -441,7 +446,9 @@
             mask = lax.broadcasted_iota(jnp.int32, (BLOCK, 128), 0) == i
             block = selfb[i].astype(F32)
             sums.append(jnp.sum(jnp.where(mask, block, 0.0), axis=0, keepdims=True))
-            selfb[i] = jnp.where(mask, 0.0, block).astype(BF16)
+            wide_blocks[0, i] = jnp.where(mask, 0.0, block)
+            wide_blocks[1, i] = linkb[0, i].astype(F32)
+            wide_blocks[2, i] = linkb[1, i].astype(F32)
         diag[pl.ds(pl.multiple_of(t * 8, 8), 8), :] = jnp.concatenate(sums, axis=0)
         return carry
 
@@ -456,15 +463,19 @@
     for k in FAR_FIRST + (0,):
         scatter_start(1, k)
     take_edges(0, 0, (ext.at[0], inv))
+    prepare(own_planes)
     scatter_on(0, 0)
+    plain_sweeps(True)
 
     sum_a, sum_b = scatter_done(0)
     first_wall = near[0, WIDTH]
     source_start(0, sum_a - sum_b * first_wall)
     z_arrived(0, 2)
     take_edges(0, 1, (ext.at[0], inv))
-    prepare()
-    plain_sweeps()
+    prepare(ghost_planes)
+    plain_sweeps(False)
+    for k in FAR_FIRST + (0,):
+        scatter_on(1, k)
     spread_source = source_done(0)
     two, three, wall_part = first_sweeps(spread_source)
     second_wall = plain[0] + wall_part
@@ -476,8 +487,6 @@
     for p in range(1, 4):
         near[2, WIDTH + p] = plain[p] + upper[p - 1]
     send_low(1)
-    for k in FAR_FIRST + (0,):
-        scatter_on(1, k)
     for p in range(4, cx - 3):
         near[2, WIDTH + p] = plain[p]
 
@@ -499,22 +508,23 @@
     state[...] = state[...] + upd[...]
     wide_arrived(1)
     take_edges(1, 0, (ext.at[0],))
+    keep_inside(own_planes)
+    plain_sweeps(True)
     spread_source = source_done(1)
     two, three, wall_part = first_sweeps(spread_source)
     upper = last_sweeps(1, spread_source, two, three)
 
     cool(1)
     newton_start()
+    newton_step()
     take_edges(1, 1, (ext.at[0],))
-    for p in range(planes):
-        ext[0, p] = jnp.where(inv[p] > 0.0, ext[0, p], 0.0)
-    plain_sweeps()
+    keep_inside(ghost_planes)
+    plain_sweeps(False)
     out_field[0] = plain[0] + wall_part
     for p in range(1, 4):
         out_field[p] = plain[p] + upper[p - 1]
     for p in range(4, cx - 3):
         out_field[p] = plain[p]
-    newton_step()
     lower_arrived(1)
     for p in range(3):
         out_field[cx - 3 + p] = plain[cx - 3 + p] + lower_in[1, p]
@@ -579,6 +589,7 @@
         scratch_shapes=[
             pltpu.VMEM(self_blocks.shape, BF16),
             pltpu.VMEM(link_blocks.shape, BF16),
+            scratch(3, *self_blocks.shape),
             scratch(ITERS, 4, 8, 16, 128),
             scratch(2, 4, 8, 2, 16, 128),
             scratch(2, 4, 8, 2, 16, 128),

time: 58.1 us -> 58.6 us (level)
  no operation moved by 1% of the time
where the time goes in v5:
time: 58.6 us; the launch traced here: 58.4 us
  Pallas kernels  55.9 us (95%)
  local copies, waits for them, and re-layouts  1.89 us (3%)
  between operations  0.64 us (1%)
    pallas_call x1, Pallas kernels, per_device(): pl.pallas_call(kernel, out_shape=(pltpu.VMEM(mold_temp.shape, F32), pltpu...  55.9 us
    unnamed x3, local copies, waits for them, and re-layouts  1.89 us

profile of v5, /device:TPU:7, one launch (start us, length us, event | category | flops | bytes accessed | tf_op | source)
XLA Modules:
  0.0 58.4 jit_solution(7039094950231855150)
XLA Ops:
  0.6 55.9 %shard_map.139 = (f32[16,16,128]{2,1,0:T(8,128)S(1)}, f32[64,128]{1,0:T(8,128)S(1)}, f32[64,128]{1,0:T(8,128)S(1)}) custom-call(f32[16,16,128]{2,1,0:T(8,128)} %mold.1, f32[16,16,128]{2,1,0:T(8,128)} %cap.1, f32[64,128]{1,0:T(8,128)} %melt_in.1, f32[64,128]{1,0:T(8,128)} %logp.1, f32[64,128]{1,0:T(8,128)} %target_in.1, f32[64,128]{1,0:T(8,128)} %inflow_in.1, ...), custom_call_target="tpu_custom_call" | custom-call | tf_op jit(solution)/shard_map/pallas_call | solution.py:580
  56.5 0.7 %copy.18 = f32[16,16,128]{2,1,0:T(8,128)} copy(f32[16,16,128]{2,1,0:T(8,128)S(1)} %get-tuple-element.3) | data formatting | bytes 262144
  57.2 0.6 %copy.19 = f32[64,128]{1,0:T(8,128)} copy(f32[64,128]{1,0:T(8,128)S(1)} %get-tuple-element.4) | data formatting | bytes 65536
  57.8 0.6 %copy.20 = f32[64,128]{1,0:T(8,128)} copy(f32[64,128]{1,0:T(8,128)S(1)} %get-tuple-element.5) | data formatting | bytes 65536

commit v6 on v5

--- a/solution.py
+++ b/solution.py
@@ -189,9 +189,8 @@
         ).start()
 
     def send_high(g):
-        remote(
-            near.at[group(g), pl.ds(cx, WIDTH)], near.at[group(g), pl.ds(0, WIDTH)], h_sems(g, 0, 1), beside(1, 0, 0)
-        ).start()
+        src = near.at[group(0), pl.ds(cx, WIDTH)] if g == 0 else plain.at[pl.ds(0, 1), pl.ds(cx - WIDTH, WIDTH)]
+        remote(src, near.at[group(g), pl.ds(0, WIDTH)], h_sems(g, 0, 1), beside(1, 0, 0)).start()
 
     def pack_edges(g, step):
         which, row_out, lane_out = ((own_planes, row_own, lane_own), (ghost_planes, row_ghost, lane_ghost))[step]
@@ -251,6 +250,9 @@
     def wide_arrived(g):
         wait_recv(near.at[group(g), pl.ds(WIDTH + cx, WIDTH)], h_sems(g, 0, 0))
         wait_recv(near.at[group(g), pl.ds(0, WIDTH)], h_sems(g, 0, 1))
+        if g == 1:
+            for p in range(3):
+                near[2, p + 1] = near[2, p + 1] + lower[0, p]
         pack_edges(g, 1)
         send_edges(g, 1)
 
@@ -281,7 +283,7 @@
         rows = pltpu.roll(plane, 1, 0) + pltpu.roll(plane, 23, 0)
         return rows + (pltpu.roll(plane, 1, 1) + pltpu.roll(plane, 2 * cz - 1, 1))
 
-    def plain_sweeps(inner):
+    def plain_sweeps(it, inner):
         for k in range(SWEEPS):
             now, later = k % 2, (k + 1) % 2
             edge = k + 1
@@ -290,7 +292,7 @@
                 total = (ext[now, p - 1] + ext[now, p + 1]) + around(ext[now, p]) + base[p]
                 new = total * inv[p]
                 if k == SWEEPS - 1:
-                    plain[p - WIDTH] = new[:cy, :cz]
+                    plain[it, p - WIDTH] = new[:cy, :cz]
                 else:
                     ext[later, p] = new
 
@@ -465,7 +467,7 @@
     take_edges(0, 0, (ext.at[0], inv))
     prepare(own_planes)
     scatter_on(0, 0)
-    plain_sweeps(True)
+    plain_sweeps(0, True)
 
     sum_a, sum_b = scatter_done(0)
     first_wall = near[0, WIDTH]
@@ -473,61 +475,61 @@
     z_arrived(0, 2)
     take_edges(0, 1, (ext.at[0], inv))
     prepare(ghost_planes)
-    plain_sweeps(False)
+    plain_sweeps(0, False)
+    send_high(1)
     for k in FAR_FIRST + (0,):
         scatter_on(1, k)
     spread_source = source_done(0)
     two, three, wall_part = first_sweeps(spread_source)
-    second_wall = plain[0] + wall_part
+    second_wall = plain[0, 0] + wall_part
     tab[1, 0, 0] = second_wall
     gather_start(1)
     gather_on(1, 0)
     upper = last_sweeps(0, spread_source, two, three)
     near[2, WIDTH] = second_wall
     for p in range(1, 4):
-        near[2, WIDTH + p] = plain[p] + upper[p - 1]
+        near[2, WIDTH + p] = plain[0, p] + upper[p - 1]
     send_low(1)
     for p in range(4, cx - 3):
-        near[2, WIDTH + p] = plain[p]
+        near[2, WIDTH + p] = plain[0, p]
 
     cool(0)
     newton_start()
     z_arrived(1, 1)
     z_arrived(1, 3)
+    sum_c, sum_d = scatter_done(1)
+    source_start(1, sum_a - COOLING * sum_c + COOLING * sum_d * first_wall - sum_b * second_wall)
     lower_arrived(0)
     for p in range(3):
-        near[2, WIDTH + cx - 3 + p] = plain[cx - 3 + p] + lower_in[0, p]
-    send_high(1)
+        near[2, WIDTH + cx - 3 + p] = plain[0, cx - 3 + p] + lower_in[0, p]
     pack_edges(1, 0)
     send_edges(1, 0)
     newton_step()
-    sum_c, sum_d = scatter_done(1)
-    source_start(1, sum_a - COOLING * sum_c + COOLING * sum_d * first_wall - sum_b * second_wall)
     z_arrived(1, 2)
+    wide_arrived(1)
     newton_step()
     state[...] = state[...] + upd[...]
-    wide_arrived(1)
-    take_edges(1, 0, (ext.at[0],))
-    keep_inside(own_planes)
-    plain_sweeps(True)
     spread_source = source_done(1)
     two, three, wall_part = first_sweeps(spread_source)
     upper = last_sweeps(1, spread_source, two, three)
+    take_edges(1, 0, (ext.at[0],))
+    keep_inside(own_planes)
+    plain_sweeps(1, True)
 
     cool(1)
     newton_start()
-    newton_step()
     take_edges(1, 1, (ext.at[0],))
     keep_inside(ghost_planes)
-    plain_sweeps(False)
-    out_field[0] = plain[0] + wall_part
+    plain_sweeps(1, False)
+    out_field[0] = plain[1, 0] + wall_part
     for p in range(1, 4):
-        out_field[p] = plain[p] + upper[p - 1]
+        out_field[p] = plain[1, p] + upper[p - 1]
     for p in range(4, cx - 3):
-        out_field[p] = plain[p]
+        out_field[p] = plain[1, p]
+    newton_step()
     lower_arrived(1)
     for p in range(3):
-        out_field[cx - 3 + p] = plain[cx - 3 + p] + lower_in[1, p]
+        out_field[cx - 3 + p] = plain[1, cx - 3 + p] + lower_in[1, p]
     newton_step()
     mt, st = melt[...], state[...] + upd[...]
     out_press[...] = BULK_BASE * jnp.exp(-BULK_SLOPE * mt) * (jnp.exp(st) - 1.0)
@@ -609,7 +611,7 @@
             scratch(2, planes, 24, 2 * cz),
             scratch(planes, 24, 2 * cz),
             scratch(planes, 24, 2 * cz),
-            scratch(cx, cy, cz),
+            scratch(ITERS, cx, cy, cz),
             scratch(ITERS, 2, 8, cz),
             scratch(ITERS, 10, 8, cz),
             scratch(ITERS, 3, cy, cz),

time: 58.6 us -> 53.5 us (0.913)
  Pallas kernels: 55.9 us -> 50.6 us
    pallas_call x1, Pallas kernels: 55.9 us -> 50.6 us  [per_device(): pl.pallas_call(kernel, out_shape=(pltpu.VMEM(mold_temp.shape, F32), pltpu...]
where the time goes in v6:
time: 53.5 us; the launch traced here: 53.1 us
  Pallas kernels  50.6 us (95%)
  local copies, waits for them, and re-layouts  1.89 us (4%)
  between operations  0.64 us (1%)
    pallas_call x1, Pallas kernels, per_device(): pl.pallas_call(kernel, out_shape=(pltpu.VMEM(mold_temp.shape, F32), pltpu...  50.6 us
    unnamed x3, local copies, waits for them, and re-layouts  1.89 us

profile of v6, /device:TPU:7, one launch (start us, length us, event | category | flops | bytes accessed | tf_op | source)
XLA Modules:
  0.0 53.1 jit_solution(4449332341034192349)
XLA Ops:
  0.6 50.6 %shard_map.139 = (f32[16,16,128]{2,1,0:T(8,128)S(1)}, f32[64,128]{1,0:T(8,128)S(1)}, f32[64,128]{1,0:T(8,128)S(1)}) custom-call(f32[16,16,128]{2,1,0:T(8,128)} %mold.1, f32[16,16,128]{2,1,0:T(8,128)} %cap.1, f32[64,128]{1,0:T(8,128)} %melt_in.1, f32[64,128]{1,0:T(8,128)} %logp.1, f32[64,128]{1,0:T(8,128)} %target_in.1, f32[64,128]{1,0:T(8,128)} %inflow_in.1, ...), custom_call_target="tpu_custom_call" | custom-call | tf_op jit(solution)/shard_map/pallas_call | solution.py:582
  51.2 0.7 %copy.18 = f32[16,16,128]{2,1,0:T(8,128)} copy(f32[16,16,128]{2,1,0:T(8,128)S(1)} %get-tuple-element.3) | data formatting | bytes 262144
  51.9 0.6 %copy.19 = f32[64,128]{1,0:T(8,128)} copy(f32[64,128]{1,0:T(8,128)S(1)} %get-tuple-element.4) | data formatting | bytes 65536
  52.5 0.6 %copy.20 = f32[64,128]{1,0:T(8,128)} copy(f32[64,128]{1,0:T(8,128)S(1)} %get-tuple-element.5) | data formatting | bytes 65536

commit v7 on v6

--- a/solution.py
+++ b/solution.py
@@ -133,6 +133,8 @@
     def sum_sems(a, k):
         return (ysend_sem.at[a, k], yrecv_sem.at[a, k])
 
+    sums = (pl.ds(0, 2), pl.ds(0, 1))
+
     def scatter_terms(values):
         parts = []
         for value in values:
@@ -155,18 +157,25 @@
 
     def scatter_on(a, k):
         wait_recv(rs1.at[a, k, pl.ds(1, 7)], scatter_sems(a, k))
+        totals = []
         for q in range(2):
             total = spread[a, k, 0, q]
             for j in range(1, 8):
                 total = total + rs1[a, k, j, q]
-            psum[a, k, q] = total
+            totals.append(total)
+        if a == 0:
+            psum[a, k, 0], psum[a, k, 1] = totals
+        else:
+            psum[a, k, 0] = COOLING * (totals[0] - totals[1] * tab[0, k, 0])
         if k > 0:
-            remote(psum.at[a, k], rs2.at[a, k], sum_sems(a, k), z_peer(k)).start()
+            remote(psum.at[a, k, sums[a]], rs2.at[a, k, sums[a]], sum_sems(a, k), z_peer(k)).start()
 
     def scatter_done(a):
         for k in (1, 3, 2):
-            wait_recv(rs2.at[a, k], sum_sems(a, k))
-        return [((psum[a, 0, q] + rs2[a, 1, q]) + (rs2[a, 3, q] + rs2[a, 2, q])) for q in range(2)]
+            wait_recv(rs2.at[a, k, sums[a]], sum_sems(a, k))
+        return [
+            ((psum[a, 0, q] + rs2[a, 1, q]) + (rs2[a, 3, q] + rs2[a, 2, q])) for q in range(2 - a)
+        ]
 
     lane = lax.broadcasted_iota(jnp.int32, (cy, cz), 1)
     lane24 = lax.broadcasted_iota(jnp.int32, (24, cz), 1)
@@ -433,7 +442,10 @@
     gather_start(0)
     send_edges(0, 0)
     scatter_start(0, 0)
-    gather_on(0, 0)
+    square = coef[...] * coef[...]
+    scatter_fill(1, scatter_terms((square * melt[...], square)))
+    for k in FAR_FIRST + (0,):
+        scatter_start(1, k)
     hot_t[...] = hot32.T.astype(BF16)
     for load in loads[6:]:
         load.wait()
@@ -457,13 +469,10 @@
     lax.fori_loop(0, BLOCK // 8, pick, 0)
     for k in FAR_FIRST:
         scatter_on(0, k)
-    square = coef[...] * coef[...]
-    scatter_fill(1, scatter_terms((square * melt[...], square)))
+    gather_on(0, 0)
     z_arrived(0, 1)
     z_arrived(0, 3)
     wide_arrived(0)
-    for k in FAR_FIRST + (0,):
-        scatter_start(1, k)
     take_edges(0, 0, (ext.at[0], inv))
     prepare(own_planes)
     scatter_on(0, 0)
@@ -497,8 +506,8 @@
     newton_start()
     z_arrived(1, 1)
     z_arrived(1, 3)
-    sum_c, sum_d = scatter_done(1)
-    source_start(1, sum_a - COOLING * sum_c + COOLING * sum_d * first_wall - sum_b * second_wall)
+    (cooled,) = scatter_done(1)
+    source_start(1, (sum_a - cooled) - sum_b * second_wall)
     lower_arrived(0)
     for p in range(3):
         near[2, WIDTH + cx - 3 + p] = plain[0, cx - 3 + p] + lower_in[0, p]
@@ -542,7 +551,7 @@
         for k in range(4):
             if k > 0:
                 wait_send(tab.at[it, k, 0], z_sems(it, k))
-                wait_send(psum.at[it, k], sum_sems(it, k))
+                wait_send(psum.at[it, k, sums[it]], sum_sems(it, k))
             wait_send(tab.at[it, k, pl.ds(1, 7)], gather_sems(it, k))
             wait_send(spread.at[it, k, pl.ds(1, 7)], scatter_sems(it, k))
         wait_send(src_in.at[it, pl.ds(0, 2)], edge_sems(it, 0))
@@ -563,6 +572,17 @@
         for step, regions in ((0, (rows_own, lanes_own, corner_own)), (1, (rows_ghost, lanes_ghost, corner_ghost))):
             for kind, region in enumerate(regions):
                 wait_send(region.at[some], h_sems(g, step, 2 + kind))
+
+
+def store(field, press, shrink, out_field, out_press, out_shrink, sem):
+    copies = [
+        pltpu.make_async_copy(src, dst, sem.at[i])
+        for i, (src, dst) in enumerate(((field, out_field), (press, out_press), (shrink, out_shrink)))
+    ]
+    for copy in copies:
+        copy.start()
+    for copy in copies:
+        copy.wait()
 
 
 def per_device(
@@ -579,7 +599,7 @@
         return pltpu.VMEM(shape, F32)
 
     cav = scratch(cells, blocks)
-    return pl.pallas_call(
+    results = pl.pallas_call(
         kernel,
         out_shape=(
             pltpu.VMEM(mold_temp.shape, F32),
@@ -636,6 +656,14 @@
         mold_temp, capacity, melt_temp, log_pressure, target_volume, inflow, transfer_coef,
         link_columns, wall_owner.reshape(1, blocks), wall_slot.reshape(1, blocks), self_blocks, link_blocks,
     )
+    anywhere = pl.BlockSpec(memory_space=pl.ANY)
+    return pl.pallas_call(
+        store,
+        out_shape=[pltpu.HBM(result.shape, F32) for result in results],
+        in_specs=[anywhere] * 3,
+        out_specs=[anywhere] * 3,
+        scratch_shapes=[pltpu.SemaphoreType.DMA((3,))],
+    )(*results)
 
 
 def solution(mesh):

time: 53.5 us -> 60.3 us (1.13)
  the two profiles are of different devices: /device:TPU:7 before, /device:TPU:1 now
where the time goes in v7:
time: 60.3 us; the launch traced here: 60.2 us
  Pallas kernels  57.7 us (96%)
  local copies, waits for them, and re-layouts  1.84 us (3%)
  between operations  0.65 us (1%)
    pallas_call x1, Pallas kernels, per_device(): pl.pallas_call(kernel, out_shape=(pltpu.VMEM(mold_temp.shape, F32), pltpu...  50.6 us
    pallas_call x1, Pallas kernels, per_device(): pl.pallas_call(store, out_shape=[pltpu.HBM(result.shape, F32) for result...  7.08 us
    unnamed x6, local copies, waits for them, and re-layouts  1.84 us

profile of v7, /device:TPU:1, one launch (start us, length us, event | category | flops | bytes accessed | tf_op | source)
XLA Modules:
  0.0 60.2 jit_solution(13164224403861266397)
XLA Ops:
  0.6 50.6 %shard_map.139 = (f32[16,16,128]{2,1,0:T(8,128)S(1)}, f32[64,128]{1,0:T(8,128)S(1)}, f32[64,128]{1,0:T(8,128)S(1)}) custom-call(f32[16,16,128]{2,1,0:T(8,128)} %mold.1, f32[16,16,128]{2,1,0:T(8,128)} %cap.1, f32[64,128]{1,0:T(8,128)} %melt_in.1, f32[64,128]{1,0:T(8,128)} %logp.1, f32[64,128]{1,0:T(8,128)} %target_in.1, f32[64,128]{1,0:T(8,128)} %inflow_in.1, ...), custom_call_target="tpu_custom_call" | custom-call | tf_op jit(solution)/shard_map/pallas_call | solution.py:602
  51.3 0.0 copy-start
  51.3 0.6 %copy-done = f32[16,16,128]{2,1,0:T(8,128)} copy-done((f32[16,16,128]{2,1,0:T(8,128)}, f32[16,16,128]{2,1,0:T(8,128)S(1)}, u32[]{:S(2)}) %copy-start) | copy-done | bytes 131096
  51.9 0.0 copy-start.1
  51.9 0.6 copy-done.1
  52.5 0.0 copy-start.2
  52.5 0.6 %copy-done.2 = f32[64,128]{1,0:T(8,128)} copy-done((f32[64,128]{1,0:T(8,128)}, f32[64,128]{1,0:T(8,128)S(1)}, u32[]{:S(2)}) %copy-start.2) | copy-done | bytes 32792
  53.1 7.1 %shard_map.140 = (f32[16,16,128]{2,1,0:T(8,128)}, f32[64,128]{1,0:T(8,128)}, f32[64,128]{1,0:T(8,128)}) custom-call(f32[16,16,128]{2,1,0:T(8,128)} %copy-done, f32[64,128]{1,0:T(8,128)} %copy-done.1, f32[64,128]{1,0:T(8,128)} %copy-done.2), custom_call_target="tpu_custom_call" | custom-call | tf_op jit(solution)/shard_map/pallas_call | solution.py:660
Async XLA Ops:
  51.3 0.6 %copy-start = (f32[16,16,128]{2,1,0:T(8,128)}, f32[16,16,128]{2,1,0:T(8,128)S(1)}, u32[]{:S(2)}) copy-start(f32[16,16,128]{2,1,0:T(8,128)S(1)} %get-tuple-element.6.field) | copy-start | bytes 393220
  51.9 0.6 copy-start.1
  52.5 0.6 %copy-start.2 = (f32[64,128]{1,0:T(8,128)}, f32[64,128]{1,0:T(8,128)S(1)}, u32[]{:S(2)}) copy-start(f32[64,128]{1,0:T(8,128)S(1)} %get-tuple-element.8.shrink) | copy-start | bytes 98308

commit v8 on v7

--- a/solution.py
+++ b/solution.py
@@ -13,6 +13,7 @@
 INNER = 2
 WIDTH = 4
 FAR_FIRST = (2, 1, 3)
+TWO_HOPS_FIRST = (4, 5, 2, 3, 6, 7, 1)
 
 CONDUCT = 1.0
 COOLING = 0.5
@@ -44,7 +45,7 @@
 
 def kernel(
     mold, cap, melt_in, logp, target_in, inflow_in, coef_in, columns_in, owner_in, slot_in, self_in, link_in,
-    out_field, out_press, out_shrink,
+    out_field, out_melt, out_state,
     selfb, linkb, wide_blocks, tab, spread, rs1, psum, rs2, near,
     row_own, row_ghost, lane_own, lane_ghost, rows_own, rows_ghost, lanes_own, lanes_ghost, corner_own, corner_ghost,
     ext, inv, base, plain, srcb, src_in, lower, lower_in,
@@ -104,7 +105,7 @@
         return (gsend_sem.at[it, k], grecv_sem.at[it, k])
 
     def gather_on(it, k):
-        for j in range(1, 8):
+        for j in TWO_HOPS_FIRST:
             remote(tab.at[it, k, 0], tab.at[it, k, j], gather_sems(it, k), xc_peer(j)).start()
 
     def gather_start(it):
@@ -152,7 +153,7 @@
                 spread[a, k, :, q] = one.reshape(8, 16, 128)
 
     def scatter_start(a, k):
-        for j in range(1, 8):
+        for j in TWO_HOPS_FIRST:
             remote(spread.at[a, k, j], rs1.at[a, k, j], scatter_sems(a, k), xc_peer(j)).start()
 
     def scatter_on(a, k):
@@ -418,6 +419,34 @@
         weighted = (slope[...] * upd[...]).astype(BF16)
         upd[...] = (-resid[...] - apply(weighted)) / jdiag[...]
 
+    def sends_left(it):
+        def wait_send(region, sems):
+            remote(region, region, sems, beside(0, 1, 0)).wait_send()
+
+        for k in range(4):
+            if k > 0:
+                wait_send(tab.at[it, k, 0], z_sems(it, k))
+                wait_send(psum.at[it, k, sums[it]], sum_sems(it, k))
+            wait_send(tab.at[it, k, pl.ds(1, 7)], gather_sems(it, k))
+            wait_send(spread.at[it, k, pl.ds(1, 7)], scatter_sems(it, k))
+        wait_send(src_in.at[it, pl.ds(0, 2)], edge_sems(it, 0))
+
+        @pl.when(n > 0)
+        def _():
+            wait_send(src_in.at[it, pl.ds(2, 4)], edge_sems(it, 1))
+
+        @pl.when(n < n_n - 1)
+        def _():
+            wait_send(src_in.at[it, pl.ds(6, 4)], edge_sems(it, 2))
+
+        wait_send(lower.at[it], (lsend_sem.at[it], lrecv_sem.at[it]))
+        some = group(it)
+        wait_send(near.at[some, pl.ds(0, WIDTH)], h_sems(it, 0, 0))
+        wait_send(near.at[some, pl.ds(0, WIDTH)], h_sems(it, 0, 1))
+        for step, regions in ((0, (rows_own, lanes_own, corner_own)), (1, (rows_ghost, lanes_ghost, corner_ghost))):
+            for kind, region in enumerate(regions):
+                wait_send(region.at[some], h_sems(it, step, 2 + kind))
+
     for load in loads[:4]:
         load.wait()
     rel = jnp.bitwise_xor(owner[...], w)
@@ -524,6 +553,7 @@
     take_edges(1, 0, (ext.at[0],))
     keep_inside(own_planes)
     plain_sweeps(1, True)
+    sends_left(0)
 
     cool(1)
     newton_start()
@@ -540,49 +570,9 @@
     for p in range(3):
         out_field[cx - 3 + p] = plain[1, cx - 3 + p] + lower_in[1, p]
     newton_step()
-    mt, st = melt[...], state[...] + upd[...]
-    out_press[...] = BULK_BASE * jnp.exp(-BULK_SLOPE * mt) * (jnp.exp(st) - 1.0)
-    out_shrink[...] = 1.0 - jnp.exp(EXPAND * mt) * (1.0 - TAIT_C * st)
-
-    def wait_send(region, sems):
-        remote(region, region, sems, beside(0, 1, 0)).wait_send()
-
-    for it in range(ITERS):
-        for k in range(4):
-            if k > 0:
-                wait_send(tab.at[it, k, 0], z_sems(it, k))
-                wait_send(psum.at[it, k, sums[it]], sum_sems(it, k))
-            wait_send(tab.at[it, k, pl.ds(1, 7)], gather_sems(it, k))
-            wait_send(spread.at[it, k, pl.ds(1, 7)], scatter_sems(it, k))
-        wait_send(src_in.at[it, pl.ds(0, 2)], edge_sems(it, 0))
-
-        @pl.when(n > 0)
-        def _():
-            wait_send(src_in.at[it, pl.ds(2, 4)], edge_sems(it, 1))
-
-        @pl.when(n < n_n - 1)
-        def _():
-            wait_send(src_in.at[it, pl.ds(6, 4)], edge_sems(it, 2))
-
-        wait_send(lower.at[it], (lsend_sem.at[it], lrecv_sem.at[it]))
-    for g in range(2):
-        some = group(g)
-        wait_send(near.at[some, pl.ds(0, WIDTH)], h_sems(g, 0, 0))
-        wait_send(near.at[some, pl.ds(0, WIDTH)], h_sems(g, 0, 1))
-        for step, regions in ((0, (rows_own, lanes_own, corner_own)), (1, (rows_ghost, lanes_ghost, corner_ghost))):
-            for kind, region in enumerate(regions):
-                wait_send(region.at[some], h_sems(g, step, 2 + kind))
-
-
-def store(field, press, shrink, out_field, out_press, out_shrink, sem):
-    copies = [
-        pltpu.make_async_copy(src, dst, sem.at[i])
-        for i, (src, dst) in enumerate(((field, out_field), (press, out_press), (shrink, out_shrink)))
-    ]
-    for copy in copies:
-        copy.start()
-    for copy in copies:
-        copy.wait()
+    out_melt[...] = melt[...]
+    out_state[...] = state[...] + upd[...]
+    sends_left(1)
 
 
 def per_device(
@@ -599,7 +589,7 @@
         return pltpu.VMEM(shape, F32)
 
     cav = scratch(cells, blocks)
-    results = pl.pallas_call(
+    field, melt, state = pl.pallas_call(
         kernel,
         out_shape=(
             pltpu.VMEM(mold_temp.shape, F32),
@@ -656,14 +646,9 @@
         mold_temp, capacity, melt_temp, log_pressure, target_volume, inflow, transfer_coef,
         link_columns, wall_owner.reshape(1, blocks), wall_slot.reshape(1, blocks), self_blocks, link_blocks,
     )
-    anywhere = pl.BlockSpec(memory_space=pl.ANY)
-    return pl.pallas_call(
-        store,
-        out_shape=[pltpu.HBM(result.shape, F32) for result in results],
-        in_specs=[anywhere] * 3,
-        out_specs=[anywhere] * 3,
-        scratch_shapes=[pltpu.SemaphoreType.DMA((3,))],
-    )(*results)
+    pressure = BULK_BASE * jnp.exp(-BULK_SLOPE * melt) * (jnp.exp(state) - 1.0)
+    shrinkage = 1.0 - jnp.exp(EXPAND * melt) * (1.0 - TAIT_C * state)
+    return field, pressure, shrinkage
 
 
 def solution(mesh):

time: 60.3 us -> 52.9 us (0.88)
  Pallas kernels: 57.7 us -> 50.8 us
  local copies, waits for them, and re-layouts: 1.84 us -> 0.66 us
  other arithmetic: 0 us -> 0.65 us
    pallas_call x1 -> x0, Pallas kernels: 7.08 us -> none  [per_device(): pl.pallas_call(store, out_shape=[pltpu.HBM(result.shape, F32) for result...]
    unnamed x6 -> x1, local copies, waits for them, and re-layouts: 1.84 us -> 0.66 us
    sub x0 -> x1, other arithmetic: none -> 0.65 us  [per_device(): shrinkage = 1.0 - jnp.exp(EXPAND * melt) * (1.0 - TAIT_C * state)]
where the time goes in v8:
time: 52.9 us; the launch traced here: 52.8 us
  Pallas kernels  50.8 us (96%)
  local copies, waits for them, and re-layouts  0.66 us (1%)
  other arithmetic  0.65 us (1%)
  between operations  0.64 us (1%)
    pallas_call x1, Pallas kernels, per_device(): pl.pallas_call(kernel, out_shape=(pltpu.VMEM(mold_temp.shape, F32), pltpu...  50.8 us

profile of v8, /device:TPU:1, one launch (start us, length us, event | category | flops | bytes accessed | tf_op | source)
XLA Modules:
  0.0 52.8 jit_solution(17810191782088028526)
XLA Ops:
  0.6 50.8 %shard_map.139 = (f32[16,16,128]{2,1,0:T(8,128)S(1)}, f32[64,128]{1,0:T(8,128)S(1)}, f32[64,128]{1,0:T(8,128)S(1)}) custom-call(f32[16,16,128]{2,1,0:T(8,128)} %mold.1, f32[16,16,128]{2,1,0:T(8,128)} %cap.1, f32[64,128]{1,0:T(8,128)} %melt_in.1, f32[64,128]{1,0:T(8,128)} %logp.1, f32[64,128]{1,0:T(8,128)} %target_in.1, f32[64,128]{1,0:T(8,128)} %inflow_in.1, ...), custom_call_target="tpu_custom_call" | custom-call | tf_op jit(solution)/shard_map/pallas_call | solution.py:592
  51.5 0.7 %copy.16 = f32[16,16,128]{2,1,0:T(8,128)} copy(f32[16,16,128]{2,1,0:T(8,128)S(1)} %get-tuple-element.11) | data formatting | bytes 262144
  52.1 0.6 %multiply_subtract_fusion = (f32[64,128]{1,0:T(8,128)}, f32[64,128]{1,0:T(8,128)}) fusion(f32[64,128]{1,0:T(8,128)S(1)} %get-tuple-element.8, f32[64,128]{1,0:T(8,128)S(1)} %get-tuple-element.7), kind=kLoop, calls=%fused_computation | loop fusion | flops 73728 | bytes 131072 | tf_op jit(solution)/shard_map/sub | solution.py:650

commit v9 on v8

--- a/solution.py
+++ b/solution.py
@@ -71,6 +71,9 @@
     def beside(dw, dm, dn):
         return ((w + n_w + dw) % n_w, (m + n_m + dm) % n_m, (n + n_n + dn) % n_n)
 
+    for edge in (lanes_own, lanes_ghost, corner_own, corner_ghost):
+        for a in range(3):
+            edge[a] = jnp.zeros((2, 2, 8, cz), F32)
     barrier = pltpu.get_barrier_semaphore()
     peers = [z_peer(k) for k in range(1, 4)] + [xc_peer(j) for j in range(1, 8)]
     peers += [beside(-1, 0, 0), beside(1, 0, 0)]
@@ -224,20 +227,41 @@
         some = group(g)
         for side, dm in ((0, -1), (1, 1)):
             remote(row_out.at[some, side], rows_in.at[some, side], h_sems(g, step, 2), beside(0, dm, 0)).start()
-        for side, dn in ((0, -1), (1, 1)):
-            remote(lane_out.at[some], lanes_in.at[some, side], h_sems(g, step, 3), beside(0, 0, dn)).start()
+
+        def send_lanes(side, dn):
+            remote(lane_out.at[some], lanes_in.at[some, side], h_sems(g, step, 3 + 2 * side), beside(0, 0, dn)).start()
             for tile, dm in ((0, -1), (1, 1)):
                 remote(
-                    lane_out.at[some, tile], corner_in.at[some, side, tile], h_sems(g, step, 4), beside(0, dm, dn)
+                    lane_out.at[some, tile], corner_in.at[some, side, tile], h_sems(g, step, 4 + 2 * side), beside(0, dm, dn)
                 ).start()
+
+        @pl.when(n > 0)
+        def _():
+            send_lanes(0, -1)
+
+        @pl.when(n < n_n - 1)
+        def _():
+            send_lanes(1, 1)
 
     def take_edges(g, step, places):
         which, rows_in, lanes_in, corner_in = (
             (own_planes, rows_own, lanes_own, corner_own), (ghost_planes, rows_ghost, lanes_ghost, corner_ghost),
         )[step]
         some = group(g)
-        for kind, region in ((2, rows_in), (3, lanes_in), (4, corner_in)):
-            wait_recv(region.at[some], h_sems(g, step, kind))
+        wait_recv(rows_in.at[some], h_sems(g, step, 2))
+
+        def wait_lanes(side):
+            wait_recv(lanes_in.at[some, side], h_sems(g, step, 3 + 2 * side))
+            wait_recv(corner_in.at[some, side], h_sems(g, step, 4 + 2 * side))
+
+        @pl.when(n < n_n - 1)
+        def _():
+            wait_lanes(0)
+
+        @pl.when(n > 0)
+        def _():
+            wait_lanes(1)
+
         for a, dst in zip(arrays[g], places):
             sides = []
             for side in range(2):
@@ -444,8 +468,14 @@
         wait_send(near.at[some, pl.ds(0, WIDTH)], h_sems(it, 0, 0))
         wait_send(near.at[some, pl.ds(0, WIDTH)], h_sems(it, 0, 1))
         for step, regions in ((0, (rows_own, lanes_own, corner_own)), (1, (rows_ghost, lanes_ghost, corner_ghost))):
-            for kind, region in enumerate(regions):
-                wait_send(region.at[some], h_sems(it, step, 2 + kind))
+            rows, lanes, corner = regions
+            wait_send(rows.at[some], h_sems(it, step, 2))
+            for side, sent in ((0, n > 0), (1, n < n_n - 1)):
+
+                @pl.when(sent)
+                def _(step=step, lanes=lanes, corner=corner, side=side):
+                    wait_send(lanes.at[some, side], h_sems(it, step, 3 + 2 * side))
+                    wait_send(corner.at[some, side], h_sems(it, step, 4 + 2 * side))
 
     for load in loads[:4]:
         load.wait()
@@ -535,6 +565,7 @@
     newton_start()
     z_arrived(1, 1)
     z_arrived(1, 3)
+    newton_step()
     (cooled,) = scatter_done(1)
     source_start(1, (sum_a - cooled) - sum_b * second_wall)
     lower_arrived(0)
@@ -542,7 +573,6 @@
         near[2, WIDTH + cx - 3 + p] = plain[0, cx - 3 + p] + lower_in[0, p]
     pack_edges(1, 0)
     send_edges(1, 0)
-    newton_step()
     z_arrived(1, 2)
     wide_arrived(1)
     newton_step()
@@ -566,12 +596,12 @@
     for p in range(4, cx - 3):
         out_field[p] = plain[1, p]
     newton_step()
+    newton_step()
+    out_melt[...] = melt[...]
+    out_state[...] = state[...] + upd[...]
     lower_arrived(1)
     for p in range(3):
         out_field[cx - 3 + p] = plain[1, cx - 3 + p] + lower_in[1, p]
-    newton_step()
-    out_melt[...] = melt[...]
-    out_state[...] = state[...] + upd[...]
     sends_left(1)
 
 
@@ -637,7 +667,7 @@
             *[pltpu.SemaphoreType.DMA((ITERS, 4))] * 8,
             *[pltpu.SemaphoreType.DMA((ITERS, 3))] * 2,
             *[pltpu.SemaphoreType.DMA((ITERS,))] * 2,
-            *[pltpu.SemaphoreType.DMA((2, 2, 5))] * 2,
+            *[pltpu.SemaphoreType.DMA((2, 2, 7))] * 2,
         ],
         compiler_params=pltpu.CompilerParams(
             collective_id=0, has_side_effects=True, vmem_limit_bytes=56 * 1024 * 1024

time: 52.9 us -> 51.9 us (0.981)
  the two profiles are of different devices: /device:TPU:1 before, /device:TPU:7 now
where the time goes in v9:
time: 51.9 us; the launch traced here: 51.7 us
  Pallas kernels  49.8 us (96%)
  local copies, waits for them, and re-layouts  0.66 us (1%)
  other arithmetic  0.65 us (1%)
  between operations  0.64 us (1%)
    pallas_call x1, Pallas kernels, per_device(): pl.pallas_call(kernel, out_shape=(pltpu.VMEM(mold_temp.shape, F32), pltpu...  49.8 us

profile of v9, /device:TPU:7, one launch (start us, length us, event | category | flops | bytes accessed | tf_op | source)
XLA Modules:
  0.0 51.7 jit_solution(15918519232033885803)
XLA Ops:
  0.6 49.8 %shard_map.139 = (f32[16,16,128]{2,1,0:T(8,128)S(1)}, f32[64,128]{1,0:T(8,128)S(1)}, f32[64,128]{1,0:T(8,128)S(1)}) custom-call(f32[16,16,128]{2,1,0:T(8,128)} %mold.1, f32[16,16,128]{2,1,0:T(8,128)} %cap.1, f32[64,128]{1,0:T(8,128)} %melt_in.1, f32[64,128]{1,0:T(8,128)} %logp.1, f32[64,128]{1,0:T(8,128)} %target_in.1, f32[64,128]{1,0:T(8,128)} %inflow_in.1, ...), custom_call_target="tpu_custom_call" | custom-call | tf_op jit(solution)/shard_map/pallas_call | solution.py:622
  50.4 0.7 %copy.16 = f32[16,16,128]{2,1,0:T(8,128)} copy(f32[16,16,128]{2,1,0:T(8,128)S(1)} %get-tuple-element.11) | data formatting | bytes 262144
  51.1 0.6 %multiply_subtract_fusion = (f32[64,128]{1,0:T(8,128)}, f32[64,128]{1,0:T(8,128)}) fusion(f32[64,128]{1,0:T(8,128)S(1)} %get-tuple-element.8, f32[64,128]{1,0:T(8,128)S(1)} %get-tuple-element.7), kind=kLoop, calls=%fused_computation | loop fusion | flops 73728 | bytes 131072 | tf_op jit(solution)/shard_map/sub | solution.py:680

commit v10 on v9

--- a/solution.py
+++ b/solution.py
@@ -587,6 +587,11 @@
 
     cool(1)
     newton_start()
+    newton_step()
+    newton_step()
+    out_melt[...] = melt[...]
+    out_state[...] = state[...] + upd[...]
+    sends_left(1)
     take_edges(1, 1, (ext.at[0],))
     keep_inside(ghost_planes)
     plain_sweeps(1, False)
@@ -595,14 +600,9 @@
         out_field[p] = plain[1, p] + upper[p - 1]
     for p in range(4, cx - 3):
         out_field[p] = plain[1, p]
-    newton_step()
-    newton_step()
-    out_melt[...] = melt[...]
-    out_state[...] = state[...] + upd[...]
     lower_arrived(1)
     for p in range(3):
         out_field[cx - 3 + p] = plain[1, cx - 3 + p] + lower_in[1, p]
-    sends_left(1)
 
 
 def per_device(

time: 51.9 us -> 52 us (level)
  no operation moved by 1% of the time
where the time goes in v10:
time: 52 us; the launch traced here: 51.7 us
  Pallas kernels  49.7 us (96%)
  local copies, waits for them, and re-layouts  0.66 us (1%)
  other arithmetic  0.65 us (1%)
  between operations  0.64 us (1%)
    pallas_call x1, Pallas kernels, per_device(): pl.pallas_call(kernel, out_shape=(pltpu.VMEM(mold_temp.shape, F32), pltpu...  49.7 us

profile of v10, /device:TPU:7, one launch (start us, length us, event | category | flops | bytes accessed | tf_op | source)
XLA Modules:
  0.0 51.7 jit_solution(11093088954854033015)
XLA Ops:
  0.6 49.7 %shard_map.139 = (f32[16,16,128]{2,1,0:T(8,128)S(1)}, f32[64,128]{1,0:T(8,128)S(1)}, f32[64,128]{1,0:T(8,128)S(1)}) custom-call(f32[16,16,128]{2,1,0:T(8,128)} %mold.1, f32[16,16,128]{2,1,0:T(8,128)} %cap.1, f32[64,128]{1,0:T(8,128)} %melt_in.1, f32[64,128]{1,0:T(8,128)} %logp.1, f32[64,128]{1,0:T(8,128)} %target_in.1, f32[64,128]{1,0:T(8,128)} %inflow_in.1, ...), custom_call_target="tpu_custom_call" | custom-call | tf_op jit(solution)/shard_map/pallas_call | solution.py:622
  50.4 0.7 %copy.16 = f32[16,16,128]{2,1,0:T(8,128)} copy(f32[16,16,128]{2,1,0:T(8,128)S(1)} %get-tuple-element.11) | data formatting | bytes 262144
  51.0 0.6 %multiply_subtract_fusion = (f32[64,128]{1,0:T(8,128)}, f32[64,128]{1,0:T(8,128)}) fusion(f32[64,128]{1,0:T(8,128)S(1)} %get-tuple-element.8, f32[64,128]{1,0:T(8,128)S(1)} %get-tuple-element.7), kind=kLoop, calls=%fused_computation | loop fusion | flops 73728 | bytes 131072 | tf_op jit(solution)/shard_map/sub | solution.py:680
